TPU v7x, 256 devices: a whole 4x4x8 slice. The times are simulated.
256 devices in a mesh: station: 16 (over z, y_hi), group: 8 (over x, core), bias: 2 (over y_lo).
Axes of the slice: x: 4, y: 4 (y_hi: 2, y_lo: 2; y = y_hi * 2 + y_lo), z: 8, core: 2. Of those that a mesh axis runs over, the one named last changes fastest.
Arguments:
- normal_mat: float32 [1024, 2304], P(('station', 'group')), may hold values from -16 to 18, as said below
- coupling: float32 [1024, 2, 8, 48, 128], P(('station', 'group'), 'bias'), may hold values from -0.13258252 to 0.13258252
- lengths: int32 [1024], P(('station', 'group')), may hold values from 12 to 48
- visible: int32 [1024, 2, 8], P(('station', 'group'), 'bias'), may hold values from 0 to 16, as said below
- bias_prior: float32 [2, 16, 128], P('bias', 'station'), may hold values from 0.1 to 1
- unimod: int32 [1024, 2304], P(('station', 'group')), may hold values from -1 to 2, as said below
Outputs:
- bias_cov: float32 [2, 16, 128, 128], P('bias', 'station')
- amb_cov: float32 [1024, 2304], P(('station', 'group'))
Inputs may be any that keep to these rules, and one draw needn't show every extreme that they name: `normal_mat`: each station's matrix, read as 48 x 48 row by row, is symmetric with all eigenvalues 1 or more. Each list visible[s, h] holds distinct block numbers below 16 in its first slots and the value 16 in its unused slots; every list has at least one block; in every draw the stations of some devices use all 8 slots. `unimod`: each station's matrix, read as 48 x 48 row by row, is a unit lower triangular times a unit upper triangular integer matrix; each row of the lower factor and each column of the upper factor holds at most one entry off the diagonal, -1 or 1; so every leading square block has determinant 1.
All inputs are finite; a program needn't handle non-finite values.
Results may differ from a plain program's by a relative error of at most 0.0003.
Values sent between devices are 32-bit elements; how exact they have to be, the bound alone decides.
A program may use at most 64 MiB of HBM per device.

v0:
```python
import jax
import jax.numpy as jnp
from jax import lax
from jax.sharding import PartitionSpec as P

NHALF = 16


precise = lax.Precision.HIGHEST


def split_up(value, dim, length):
    shape = value.shape
    blocks = value.reshape(*shape[:dim], length, shape[dim] // length, *shape[dim + 1 :])
    return jnp.moveaxis(blocks, dim, 0)


def summed_on_arrival(value, axis, dim):
    blocks = split_up(value, dim, lax.axis_size(axis))
    arrived = lax.all_to_all(blocks, axis, split_axis=0, concat_axis=0, tiled=True)
    return arrived.sum(axis=0)


def from_everyone(value, axis):
    copies = jnp.broadcast_to(value, (lax.axis_size(axis), *value.shape))
    return lax.all_to_all(copies, axis, split_axis=0, concat_axis=0, tiled=True)


def over_copies(value, axis):
    return from_everyone(value, axis).sum(axis=0)


def joined_along(blocks, dim):
    blocks = jnp.moveaxis(blocks, 0, dim)
    shape = blocks.shape
    return blocks.reshape(*shape[:dim], shape[dim] * shape[dim + 1], *shape[dim + 2 :])


def gather_directly(value, axis, dim):
    return joined_along(from_everyone(value, axis), dim)


def gathered_total(value, axis):
    blocks = lax.all_gather(value, axis)
    return blocks.sum(axis=0)


def spd_inverse(matrix):
    matrix_order = matrix.shape[-1]
    factor = jnp.linalg.cholesky(matrix)
    identity = jnp.broadcast_to(jnp.eye(matrix_order, dtype=matrix.dtype), matrix.shape)
    lower_inv = lax.linalg.triangular_solve(factor, identity, left_side=True, lower=True)
    return jnp.einsum("...ka,...kb->...ab", lower_inv, lower_inv, precision=precise)


def prepare(normal_mat, coupling, lengths):
    stations = coupling.shape[0]
    block_len = coupling.shape[3]
    positions = jnp.arange(block_len, dtype=jnp.int32)
    row_valid = (positions[None, :] < lengths[:, None]).astype(jnp.float32)
    keep_mask = row_valid[:, :, None] * row_valid[:, None, :]
    stacked = normal_mat.reshape(stations, block_len, block_len)
    effective = keep_mask * stacked + (1.0 - keep_mask) * jnp.eye(block_len, dtype=jnp.float32)
    inverse = spd_inverse(effective)
    weighted = coupling * row_valid[:, None, None, :, None]
    solved = jnp.einsum("sab,shjbc->shjac", inverse, weighted, precision=precise)
    return (keep_mask, inverse, weighted, solved)


def finish_cov(keep_mask, inverse, bias_part, unimod):
    stations = keep_mask.shape[0]
    block_len = keep_mask.shape[1]
    covariance = keep_mask * (inverse + bias_part)
    integer_map = unimod.reshape(stations, block_len, block_len).astype(jnp.float32)
    mapped = jnp.einsum("sab,sbc,sdc->sad", integer_map, covariance, integer_map, precision=precise)
    return (keep_mask * mapped).reshape(stations, block_len * block_len)


def local(normal_mat, coupling, lengths, visible, bias_prior, unimod):
    keep_mask, inverse, weighted, solved = prepare(normal_mat, coupling, lengths)
    reduced = jnp.einsum("shjac,shjad->shjcd", weighted, weighted - solved, precision=precise)
    block_width = coupling.shape[4]
    identity = jnp.eye(block_width, dtype=jnp.float32)
    columns = jnp.arange(NHALF, dtype=jnp.int32)
    selector = (visible[..., None] == columns).astype(jnp.float32)
    block_table = jnp.einsum("shjx,shjcd->hxcd", selector, reduced, precision=precise)
    local_sum = summed_on_arrival(block_table, "station", 1)
    block_sum = over_copies(local_sum, "group")
    bias_cov = spd_inverse(block_sum + bias_prior[..., :, None] * identity)
    segment = gather_directly(bias_cov, "station", 1)
    piece_len = segment.shape[1]
    local_pick = (visible[..., None] == jnp.arange(piece_len, dtype=jnp.int32)).astype(jnp.float32)
    chosen = jnp.einsum("shjx,hxcd->shjcd", local_pick, segment, precision=precise)
    lifted = jnp.einsum("shjac,shjcd->shjad", solved, chosen, precision=precise)
    bias_part = jnp.einsum("shjad,shjbd->sab", lifted, solved, precision=precise)
    combined = gathered_total(bias_part.reshape(bias_part.shape[0], -1), "bias")
    amb_cov = finish_cov(keep_mask, inverse, combined.reshape(bias_part.shape), unimod)
    return (bias_cov, amb_cov)


def solution(mesh):
    return jax.shard_map(
        local,
        mesh=mesh,
        in_specs=(
            P(("station", "group"), None),
            P(("station", "group"), "bias", None, None, None),
            P(("station", "group")),
            P(("station", "group"), "bias", None),
            P("bias", "station", None),
            P(("station", "group"), None),
        ),
        out_specs=(P("bias", "station", None, None), P(("station", "group"), None)),
        check_vma=False,
    )
```

profile of v0, /device:TPU:1, one launch (start us, length us, event | category | flops | bytes accessed | tf_op | source)
XLA Modules:
  0.0 209.0 jit_solution(3335769567270735851)
XLA Ops:
  0.7 0.7 fusion.43
  1.5 1.0 reshape.234
  3.0 35.2 %custom-call.14 = f32[8,48,48]{2,1,0:T(8,128)S(1)} custom-call(f32[8,48,48]{2,1,0:T(8,128)S(1)} %fusion.28), custom_call_target="Cholesky" | custom-call | tf_op jit(solution)/shard_map/jit(cholesky)/cholesky | solution.py:50
  38.4 29.5 %custom-call.15 = f32[8,1,48,48]{2,3,1,0:T(8,128)S(1)} custom-call(f32[8,1,48,48]{3,2,1,0:T(8,128)S(1)} %select_bitcast_fusion), custom_call_target="InvertDiagBlocksLowerTriangular" | custom-call | tf_op jit(solution)/shard_map/triangular_solve | solution.py:52
  68.0 0.5 fusion.26
  68.5 0.5 fusion.44
  69.0 1.7 fusion.10
  70.7 6.9 %fusion.7 = f32[8,8,128,128]{3,2,1,0:T(8,128)S(1)} fusion(f32[8,8,128,48]{2,3,1,0:T(8,128)S(1)} %fusion.10, f32[8,1,8,48,128]{4,3,2,1,0:T(8,128)S(1)} %copy-done, f32[8,48]{1,0:T(8,128)S(1)} %fusion.43), kind=kOutput, calls=%fused_computation.9 | convolution fusion | flops 605159424 | bytes 7341568 | tf_op jit(solution)/shard_map/shjac,shjad->shjcd/dot_general | solution.py:81
  77.6 4.2 %fusion.12 = f32[16,1,1,128,128]{4,0,3,2,1:T(8,128)S(1)} fusion(f32[8,8,128,128]{3,2,1,0:T(8,128)S(1)} %fusion.7, s32[8,8]{1,0:T(8,128)S(1)} %bitcast.96), kind=kOutput, calls=%fused_computation.14 | convolution fusion | flops 201327616 | bytes 5243136 | tf_op jit(solution)/shard_map/shjx,shjcd->hxcd/dot_general | solution.py:86
  82.1 39.9 %all_to_all.15 = f32[16,1,1,128,128]{4,3,2,1,0:T(8,128)S(1)} all-to-all(f32[16,1,1,128,128]{4,3,2,1,0:T(8,128)S(1)} %copy.52), channel_id=1, replica_groups=mesh['station'=16,'group'=8,'bias'=2] {'station'}, dimensions={0} | all-to-all | bytes 2097152 | tf_op jit(solution)/shard_map/all_to_all | solution.py:20
  122.1 16.0 %all_to_all.16 = f32[8,1,1,128,128]{4,3,2,1,0:T(8,128)S(1)} all-to-all(f32[8,1,1,128,128]{4,3,2,1,0:T(8,128)S(1)} %broadcast_in_dim.10), channel_id=1, replica_groups=mesh['station'=16,'group'=8,'bias'=2] {'group'}, dimensions={0} | all-to-all | bytes 1048576 | tf_op jit(solution)/shard_map/all_to_all | solution.py:26
  138.4 11.7 %custom-call.16 = f32[1,1,128,128]{3,2,1,0:T(8,128)S(1)} custom-call(f32[1,1,128,128]{3,2,1,0:T(8,128)S(1)} %fusion.36), custom_call_target="Cholesky" | custom-call | tf_op jit(solution)/shard_map/jit(cholesky)/cholesky | solution.py:50
  150.1 0.6 compare_reduce_fusion.1
  150.8 0.7 fusion.33
  151.4 9.8 %custom-call.17 = f32[1,1,1,128,128]{3,4,2,1,0:T(8,128)S(1)} custom-call(f32[1,1,1,128,128]{4,3,2,1,0:T(8,128)S(1)} %fusion.33), custom_call_target="InvertDiagBlocksLowerTriangular" | custom-call | tf_op jit(solution)/shard_map/triangular_solve | solution.py:52
  161.8 1.1 broadcast_in_dim.11
  162.9 3.9 %all-to-all-start.2 = ((f32[16,1,1,128,128]{4,3,2,1,0:T(8,128)}), f32[16,1,1,128,128]{4,3,2,1,0:T(8,128)S(1)}, u32[]{:S(2)}, u32[]{:S(2)}) async-start(f32[16,1,1,128,128]{4,3,2,1,0:T(8,128)} %broadcast_in_dim.11), calls=%async_computation.2 | async-start | bytes 2097152 | tf_op jit(solution)/shard_map/all_to_all | solution.py:26
  167.1 26.2 %all-to-all-done.2 = f32[16,1,1,128,128]{4,3,2,1,0:T(8,128)S(1)} async-done(((f32[16,1,1,128,128]{4,3,2,1,0:T(8,128)}), f32[16,1,1,128,128]{4,3,2,1,0:T(8,128)S(1)}, u32[]{:S(2)}, u32[]{:S(2)}) %all-to-all-start.2) | async-done | bytes 1048608 | tf_op jit(solution)/shard_map/all_to_all | solution.py:26
  193.2 2.1 %convolution_bitcast_fusion = f32[8,8,128,128]{3,1,0,2:T(8,128)S(1)} fusion(f32[16,1,1,128,128]{4,3,2,1,0:T(8,128)S(1)} %all-to-all-done.2, s32[8,8]{1,0:T(8,128)S(1)} %bitcast.97), kind=kOutput, calls=%fused_computation.4 | convolution fusion | flops 201327616 | bytes 5243136 | tf_op jit(solution)/shard_map/shjx,hxcd->shjcd/dot_general | solution.py:93
  195.4 6.0 %fusion = f32[8,8,48,128]{3,2,1,0:T(8,128)S(1)} fusion(f32[8,8,128,48]{2,3,1,0:T(8,128)S(1)} %fusion.10, f32[8,8,128,128]{3,1,0,2:T(8,128)S(1)} %convolution_bitcast_fusion), kind=kOutput, calls=%fused_computation | convolution fusion | flops 603979776 | bytes 7340032 | tf_op jit(solution)/shard_map/shjac,shjcd->shjad/dot_general | solution.py:94
  201.3 1.6 fusion.15
  203.0 3.9 %all_gather.3 = f32[2,8,2304]{2,1,0:T(8,128)S(1)} all-gather(f32[1,8,2304]{2,1,0:T(8,128)S(1)} %all_gather_reshape.3), channel_id=1, replica_groups=mesh['station'=16,'group'=8,'bias'=2] {'bias'}, dimensions={0}, use_global_device_ids=true | all-gather | bytes 221184 | tf_op jit(solution)/shard_map/all_gather | solution.py:44
  207.2 0.5 fusion.24
  208.2 0.8 reshape.241
  (40 shorter events, 3.3 us)
Async XLA Ops:
  2.6 66.4 %copy-start = (f32[8,1,8,48,128]{4,3,2,1,0:T(8,128)S(1)}, f32[8,1,8,48,128]{4,3,2,1,0:T(8,128)}, u32[]{:S(2)}) copy-start(f32[8,1,8,48,128]{4,3,2,1,0:T(8,128)} %param.7) | copy-start | bytes 4718596
  70.7 6.9 %copy-start.3 = (s32[8,1,8]{2,1,0:T(1,128)S(1)}, s32[8,1,8]{2,1,0:T(1,128)}, u32[]{:S(2)}) copy-start(s32[8,1,8]{2,1,0:T(1,128)} %param.9) | copy-start | bytes 772
  122.0 16.1 %copy-start.4 = (f32[1,1,128]{2,1,0:T(1,128)S(1)}, f32[1,1,128]{2,1,0:T(1,128)}, u32[]{:S(2)}) copy-start(f32[1,1,128]{2,1,0:T(1,128)} %param.10) | copy-start | bytes 1540
  161.8 1.1 copy-start.1
  161.8 5.1 %copy-start.2 = (s32[8,2304]{1,0:T(8,128)S(1)}, s32[8,2304]{1,0:T(8,128)}, u32[]{:S(2)}) copy-start(s32[8,2304]{1,0:T(8,128)} %param.11) | copy-start | bytes 221188
  162.9 30.3 %all-to-all-start.2 = ((f32[16,1,1,128,128]{4,3,2,1,0:T(8,128)}), f32[16,1,1,128,128]{4,3,2,1,0:T(8,128)S(1)}, u32[]{:S(2)}, u32[]{:S(2)}) async-start(f32[16,1,1,128,128]{4,3,2,1,0:T(8,128)} %broadcast_in_dim.11), calls=%async_computation.2 | async-start | bytes 2097152 | tf_op jit(solution)/shard_map/all_to_all | solution.py:26
where the time goes:
time: 213 us; the launch traced here: 209 us
  other arithmetic  89.1 us (42%)
  blocking collectives  59.7 us (28%)
  waiting for transfers between devices  26.2 us (12%)
  matrix products  24.8 us (12%)
  local copies, waits for them, and re-layouts  4.34 us (2%)
  starting transfers between devices  3.87 us (2%)
    another operation x7, other arithmetic, spd_inverse(): factor = jnp.linalg.cholesky(matrix)  47.7 us
    another operation x5, other arithmetic, spd_inverse(): lax.linalg.triangular_solve(factor, identity, left_side=True, lower=True)  40.1 us
    all_to_all x1, blocking collectives, summed_on_arrival(): lax.all_to_all(blocks, axis, split_axis=0, concat_axis=0, tiled=True)  39.9 us
    all_to_all x1, waiting for transfers between devices, from_everyone(): return lax.all_to_all(copies, axis, split_axis=0, concat_axis=0, tiled=True)  26.2 us
    all_to_all x1, blocking collectives, from_everyone(): return lax.all_to_all(copies, axis, split_axis=0, concat_axis=0, tiled=True)  16 us
    dot_general x1, matrix products, local(): jnp.einsum('shjac,shjad->shjcd', weighted, weighted - solved, precision=p...  6.9 us
    dot_general x1, matrix products, local(): lifted = jnp.einsum('shjac,shjcd->shjad', solved, chosen, precision=precise)  5.96 us
  transfers between devices with their start and end apart: 1, of which 1 were waited for; matrix products, arithmetic and copies ran while one was open for 0% of the time, Pallas kernels for 0%

commit v1 on v0

v1 whole, which is shorter than its diff:
```python
import jax
import jax.numpy as jnp
from jax import lax
from jax.experimental import pallas as pl
from jax.experimental.pallas import tpu as pltpu
from jax.sharding import PartitionSpec as P

A = 48
BS = 128
VH = 8
S = 8
NH = 16
NST = 16
NG = 8
HALF = A // 2
MESH = pl.DeviceIdType.MESH
F32 = jnp.float32
BF16 = jnp.bfloat16
I32 = jnp.int32
VMEM_LIMIT = 48 * 1024 * 1024


def lanes_of(shape=(8, 128)):
    return lax.broadcasted_iota(I32, shape, 1)


def subs_of(shape=(8, 128)):
    return lax.broadcasted_iota(I32, shape, 0)


def pick(x, idx):
    return jnp.take_along_axis(x, idx, axis=1, mode="promise_in_bounds")


def split2(x):
    hi = x.astype(BF16)
    lo = (x - hi.astype(F32)).astype(BF16)
    return hi, lo


def inv2(m):
    (a, b), (c, d) = m
    r = 1.0 / (a * d - b * c)
    return [[d * r, -(b * r)], [-(c * r), a * r]]


def mul2(m, n):
    return [[m[i][0] * n[0][j] + m[i][1] * n[1][j] for j in range(2)] for i in range(2)]


def inv4(p):
    a = [[p[i][j] for j in range(2)] for i in range(2)]
    b = [[p[i][j + 2] for j in range(2)] for i in range(2)]
    c = [[p[i + 2][j] for j in range(2)] for i in range(2)]
    d = [[p[i + 2][j + 2] for j in range(2)] for i in range(2)]
    ai = inv2(a)
    t = mul2(ai, b)
    u = mul2(c, ai)
    ct = mul2(c, t)
    si = inv2([[d[i][j] - ct[i][j] for j in range(2)] for i in range(2)])
    ts = mul2(t, si)
    su = mul2(si, u)
    tsu = mul2(ts, u)
    out = [[None] * 4 for _ in range(4)]
    for i in range(2):
        for j in range(2):
            out[i][j] = ai[i][j] + tsu[i][j]
            out[i][j + 2] = -ts[i][j]
            out[i + 2][j] = -su[i][j]
            out[i + 2][j + 2] = si[i][j]
    return out


def scaled_rows(pinv, rows, col, k):
    inside = (col >= k) & (col < k + 4)
    rows = [jnp.where(inside, (col == k + q).astype(F32), rows[q]) for q in range(4)]
    out = []
    for q in range(4):
        out.append((pinv[q][0] * rows[0] + pinv[q][1] * rows[1]) + (pinv[q][2] * rows[2] + pinv[q][3] * rows[3]))
    return inside, out


def unpack_rows(ref, base):
    lane = lanes_of()
    vregs = [ref[:, 128 * v : 128 * (v + 1)] for v in range(18)]
    out = []
    for r in range(HALF):
        v, o = divmod(A * r, 128)

        def part(first, shift):
            head = vregs[first] if shift == 0 else pltpu.roll(vregs[first], shift, 1)
            return head

        low = part(v, (128 - o) % 128)
        high = part(v + 9, (192 - o) % 128)
        if o + A > 128:
            low = jnp.where(lane < 128 - o, low, part(v + 1, (128 - o) % 128))
            high = jnp.where(lane < 192 - o, high, part(v + 10, (192 - o) % 128))
        out.append(jnp.where(lane < 64, low, high))
    return out


def len_column(len_ref):
    sub = subs_of()
    out = jnp.zeros((8, 128), I32)
    for s in range(S):
        out = jnp.where(sub == s, len_ref[s], out)
    return out


def invert48(rows, lens):
    lane = lanes_of()
    col = lane & 63
    side = lane & 64
    m = []
    for r in range(HALF):
        row_id = jnp.where(lane < 64, r, r + HALF)
        m.append(jnp.where((row_id < lens) & (col < lens), rows[r], (col == row_id).astype(F32)))
    for k in range(0, A, 4):
        high = k >= HALF
        r0 = k % HALF
        base = 64 if high else 0
        dup = col + base
        piv = [m[r0 + q] for q in range(4)]
        p = [[pick(piv[q], jnp.full((8, 128), base + k + r, I32)) for r in range(4)] for q in range(4)]
        pinv = inv4(p)
        inside, rh = scaled_rows(pinv, [pick(piv[q], dup) for q in range(4)], col, k)
        idx = [side + (k + q) for q in range(4)]
        own_half = (lane >= 64) if high else (lane < 64)
        new = []
        for r in range(HALF):
            c = [pick(m[r], idx[q]) for q in range(4)]
            upd = (c[0] * rh[0] + c[1] * rh[1]) + (c[2] * rh[2] + c[3] * rh[3])
            v = jnp.where(inside, 0.0, m[r]) - upd
            if r0 <= r < r0 + 4:
                v = jnp.where(own_half, rh[r - r0], v)
            new.append(v)
        m = new
    return m


def to_stations(m, buf):
    for r in range(HALF):
        buf[8 * r : 8 * r + 8, :] = m[r]
        buf[8 * (r + HALF) : 8 * (r + HALF) + 8, :] = pltpu.roll(m[r], 64, 1)


def station(buf, s):
    return buf[pl.ds(s, A, stride=S), :][:, :A]


def k1_body(len_ref, vis_ref, nm_ref, cp_ref, table_ref, s_ref, inv_ref, buf, w2, v2, slot):
    for s in range(S):
        for x in range(NH + 1):
            slot[s, x] = VH
        for j in range(VH):
            slot[s, vis_ref[s, j]] = j
    lens = len_column(len_ref)
    m = invert48(unpack_rows(nm_ref, 0), lens)
    to_stations(m, buf)
    zeros = jnp.zeros((A, 2 * BS), BF16)
    for s in range(S):
        inv = station(buf, s)
        inv_ref[s] = inv
        lhs = jnp.concatenate(split2(inv), axis=0)
        keep = lax.broadcasted_iota(I32, (A, BS), 0) < len_ref[s]
        for j in range(VH):
            w = jnp.where(keep, cp_ref[s, j], 0.0)
            wp = jnp.concatenate(split2(w), axis=1)
            w2[s, j] = wp
            out = jnp.dot(lhs, wp, preferred_element_type=F32)
            out = out[:A] + out[A:]
            sol = out[:, :BS] + out[:, BS:]
            s_ref[s, j] = jnp.concatenate(split2(sol), axis=1)
            v2[s, j] = jnp.concatenate(split2(w - sol), axis=1)
        w2[s, VH] = zeros
        v2[s, VH] = zeros
        s_ref[s, VH] = zeros

    def per_block(x, carry):
        wx = jnp.concatenate([w2[s, slot[s, x]] for s in range(S)], axis=0)
        vx = jnp.concatenate([v2[s, slot[s, x]] for s in range(S)], axis=0)
        out = lax.dot_general(wx, vx, (((0,), (0,)), ((), ())), preferred_element_type=F32)
        out = out[:BS] + out[BS:]
        out = out[:, :BS] + out[:, BS:]
        for g in range(NG):
            table_ref[g, x] = out[16 * g : 16 * g + 16]
        return carry

    lax.fori_loop(0, NH, per_block, 0)


def invert128(mat):
    lane = lanes_of()
    sub = subs_of()

    def tile_step(t, m):
        m = list(m)
        for half in range(2):
            k = 8 * t + 4 * half
            o = 4 * half
            piv = m[0]
            rows = [jnp.broadcast_to(piv[o + q : o + q + 1, :], (8, 128)) for q in range(4)]
            at = [jnp.full((8, 128), 1, I32) * (k + q) for q in range(4)]
            p = [[pick(rows[q], at[r]) for r in range(4)] for q in range(4)]
            pinv = inv4(p)
            inside, rh = scaled_rows(pinv, rows, lane, k)
            new = []
            for i in range(16):
                c = [pick(m[i], at[q]) for q in range(4)]
                upd = (c[0] * rh[0] + c[1] * rh[1]) + (c[2] * rh[2] + c[3] * rh[3])
                v = jnp.where(inside, 0.0, m[i]) - upd
                if i == 0:
                    for q in range(4):
                        v = jnp.where(sub == o + q, rh[q], v)
                new.append(v)
            m = new
        return tuple(m[1:] + m[:1])

    return lax.fori_loop(0, 16, tile_step, tuple(mat))


def peer(axis, index):
    return {axis: index}


def k2_body(table_ref, prior_ref, cov_ref, call_ref, r1, part, r2, piece, blk, seg, own, s1, q1, s2, q2, s3, q3, s4, q4, s5, q5):
    me_g = lax.axis_index("group")
    me_s = lax.axis_index("station")
    gp = [lax.rem(me_g + d, NG) for d in range(1, NG)]
    sp = [lax.rem(me_s + d, NST) for d in range(1, NST)]
    barrier = pltpu.get_barrier_semaphore()
    for g in gp:
        pl.semaphore_signal(barrier, inc=1, device_id=peer("group", g), device_id_type=MESH)
    for s in sp:
        pl.semaphore_signal(barrier, inc=1, device_id=peer("station", s), device_id_type=MESH)
    pl.semaphore_wait(barrier, NG - 1 + NST - 1)

    def send(src, dst, ss, rs, axis, index):
        copy = pltpu.make_async_remote_copy(src_ref=src, dst_ref=dst, send_sem=ss, recv_sem=rs, device_id=peer(axis, index), device_id_type=MESH)
        copy.start()
        return copy

    def arrived(src, dst, ss, rs, axis, index):
        pltpu.make_async_remote_copy(src_ref=src, dst_ref=dst, send_sem=ss, recv_sem=rs, device_id=peer(axis, index), device_id_type=MESH).wait_recv()

    sent = [send(table_ref.at[g], r1.at[me_g], s1.at[g], q1.at[me_g], "group", g) for g in gp]
    total = table_ref[me_g]
    for g in gp:
        arrived(table_ref.at[g], r1.at[g], s1.at[g], q1.at[g], "group", g)
    for g in gp:
        total = total + r1[g]
    part[...] = total
    sent += [send(part.at[s], r2.at[me_s], s2.at[s], q2.at[me_s], "station", s) for s in sp]
    total = part[me_s]
    for s in sp:
        arrived(part.at[s], r2.at[s], s2.at[s], q2.at[s], "station", s)
    for s in sp:
        total = total + r2[s]
    piece[...] = total
    sent += [send(piece, blk.at[me_g], s3.at[g], q3.at[me_g], "group", g) for g in gp]
    blk[me_g] = total
    for g in gp:
        arrived(piece, blk.at[g], s3.at[g], q3.at[g], "group", g)
    lane = lanes_of()
    sub = subs_of()
    prior = jnp.broadcast_to(prior_ref[...], (8, 128))
    mat = []
    for i in range(16):
        tile = blk[i // 2, 8 * (i % 2) : 8 * (i % 2) + 8, :]
        mat.append(tile + jnp.where(lane == sub + 8 * i, prior, 0.0))
    mat = invert128(mat)
    for i in range(16):
        own[i // 2, 8 * (i % 2) : 8 * (i % 2) + 8, :] = mat[i]
        cov_ref[8 * i : 8 * i + 8, :] = mat[i]
    sent += [send(own.at[me_g], seg.at[me_s], s4.at[s], q4.at[me_s], "station", s) for s in sp]
    seg[me_s] = own[me_g]
    for s in sp:
        arrived(own.at[me_g], seg.at[s], s4.at[s], q4.at[s], "station", s)
    sent += [send(seg, call_ref.at[me_g], s5.at[g], q5.at[me_g], "group", g) for g in gp]
    call_ref[me_g] = seg[...]
    for g in gp:
        arrived(seg, call_ref.at[g], s5.at[g], q5.at[g], "group", g)
    for copy in sent:
        copy.wait_send()


def k3_body(len_ref, vis_ref, slot_ref, s_ref, call_ref, inv_ref, um_ref, out_ref, sx, lx, buf, mine, theirs, ss, rs):
    other = 1 - lax.axis_index("bias")
    barrier = pltpu.get_barrier_semaphore()
    pl.semaphore_signal(barrier, inc=1, device_id=peer("bias", other), device_id_type=MESH)

    for x in range(NH):
        sg = [s_ref[s, slot_ref[s, x]] for s in range(S)]
        c = jnp.concatenate([call_ref[g, x] for g in range(NG)], axis=0)
        c2 = jnp.concatenate(split2(c), axis=1)
        c4 = jnp.concatenate([c2, c2], axis=0)
        out = jnp.dot(jnp.concatenate(sg, axis=0), c4, preferred_element_type=F32)
        lift = out[:, :BS] + out[:, BS:]
        hi, lo = split2(lift)
        at = slice(BS * x, BS * x + BS)
        for s in range(S):
            sx[s, :A, at] = sg[s][:, :BS]
            sx[s, A:, at] = sg[s][:, BS:]
            lx[s, :A, at] = hi[A * s : A * s + A]
            lx[s, A:, at] = lo[A * s : A * s + A]
    for s in range(S):
        out = lax.dot_general(lx[s], sx[s], (((1,), (1,)), ((), ())), preferred_element_type=F32)
        out = out[:A] + out[A:]
        mine[s] = out[:, :A] + out[:, A:]
    pl.semaphore_wait(barrier, 1)
    copy = pltpu.make_async_remote_copy(src_ref=mine, dst_ref=theirs, send_sem=ss, recv_sem=rs, device_id=peer("bias", other), device_id_type=MESH)
    copy.start()
    um = unpack_rows(um_ref, 0)
    to_stations([z.astype(F32) for z in um], buf)
    zs = [station(buf, s).astype(BF16) for s in range(S)]
    copy.wait()
    ri = lax.broadcasted_iota(I32, (A, A), 0)
    ci = lax.broadcasted_iota(I32, (A, A), 1)
    for s in range(S):
        keep = (ri < len_ref[s]) & (ci < len_ref[s])
        cov = jnp.where(keep, inv_ref[s] + (mine[s] + theirs[s]), 0.0)
        hi, lo = split2(cov)
        t = jnp.dot(zs[s], hi, preferred_element_type=F32) + jnp.dot(zs[s], lo, preferred_element_type=F32)
        hi, lo = split2(t)
        nt = (((1,), (1,)), ((), ()))
        o = lax.dot_general(hi, zs[s], nt, preferred_element_type=F32) + lax.dot_general(lo, zs[s], nt, preferred_element_type=F32)
        o = jnp.where(keep, o, 0.0)
        buf[pl.ds(s, A, stride=S), :] = jnp.concatenate([o, jnp.zeros((A, 128 - A), F32)], axis=1)
    lane = lanes_of()
    acc = [None] * 18
    for i in range(A):
        v, o = divmod(A * i, 128)
        row = buf[8 * i : 8 * i + 8, :]
        row = pltpu.roll(row, o, 1) if o else row
        if o + A > 128:
            acc[v] = row * (lane >= o) if acc[v] is None else jnp.where(lane >= o, row, acc[v])
            acc[v + 1] = jnp.where(lane < o, row, 0.0)
        else:
            acc[v] = row if acc[v] is None else jnp.where(lane >= o, row, acc[v])
    for v in range(18):
        out_ref[:, 128 * v : 128 * v + 128] = acc[v]


def local(normal_mat, coupling, lengths, visible, bias_prior, unimod):
    visible = visible.reshape(S, VH)
    coupling = coupling.reshape(S, VH, A, BS)
    vm = pl.BlockSpec(memory_space=pltpu.VMEM)
    sm = pl.BlockSpec(memory_space=pltpu.SMEM)
    table, solved, inv, slot = pl.pallas_call(
        lambda l, v, n, c, t, s, i, slot, b, w2, v2: k1_body(l, v, n, c, t, s, i, b, w2, v2, slot),
        out_shape=(
            jax.ShapeDtypeStruct((NG, NH, 16, BS), F32),
            jax.ShapeDtypeStruct((S, VH + 1, A, 2 * BS), BF16),
            jax.ShapeDtypeStruct((S, A, A), F32),
            jax.ShapeDtypeStruct((S, NH + 1), I32),
        ),
        in_specs=[sm, sm, vm, vm],
        out_specs=(vm, vm, vm, sm),
        scratch_shapes=[
            pltpu.VMEM((A * S, 128), F32),
            pltpu.VMEM((S, VH + 1, A, 2 * BS), BF16),
            pltpu.VMEM((S, VH + 1, A, 2 * BS), BF16),
        ],
        compiler_params=pltpu.CompilerParams(vmem_limit_bytes=VMEM_LIMIT),
        name="local_terms",
    )(lengths, visible, normal_mat, coupling)
    dma = pltpu.SemaphoreType.DMA
    cov, call = pl.pallas_call(
        k2_body,
        out_shape=(
            jax.ShapeDtypeStruct((BS, BS), F32),
            jax.ShapeDtypeStruct((NG, NH, 16, BS), F32),
        ),
        in_specs=[vm, vm],
        out_specs=(vm, vm),
        scratch_shapes=[
            pltpu.VMEM((NG, NH, 16, BS), F32),
            pltpu.VMEM((NH, 16, BS), F32),
            pltpu.VMEM((NH, 16, BS), F32),
            pltpu.VMEM((16, BS), F32),
            pltpu.VMEM((NG, 16, BS), F32),
            pltpu.VMEM((NH, 16, BS), F32),
            pltpu.VMEM((NG, 16, BS), F32),
            dma((NG,)), dma((NG,)), dma((NST,)), dma((NST,)), dma((NG,)), dma((NG,)), dma((NST,)), dma((NST,)), dma((NG,)), dma((NG,)),
        ],
        compiler_params=pltpu.CompilerParams(vmem_limit_bytes=VMEM_LIMIT, collective_id=0, has_side_effects=True),
        name="block_cov",
    )(table, bias_prior.reshape(1, BS))
    amb = pl.pallas_call(
        k3_body,
        out_shape=jax.ShapeDtypeStruct((S, A * A), F32),
        in_specs=[sm, sm, sm, vm, vm, vm, vm],
        out_specs=vm,
        scratch_shapes=[
            pltpu.VMEM((S, 2 * A, NH * BS), BF16),
            pltpu.VMEM((S, 2 * A, NH * BS), BF16),
            pltpu.VMEM((A * S, 128), F32),
            pltpu.VMEM((S, A, A), F32),
            pltpu.VMEM((S, A, A), F32),
            dma(()), dma(()),
        ],
        compiler_params=pltpu.CompilerParams(vmem_limit_bytes=VMEM_LIMIT, collective_id=1, has_side_effects=True),
        name="amb_cov",
    )(lengths, visible, slot, solved, call, inv, unimod)
    return (cov.reshape(1, 1, BS, BS), amb)


def solution(mesh):
    return jax.shard_map(
        local,
        mesh=mesh,
        in_specs=(
            P(("station", "group"), None),
            P(("station", "group"), "bias", None, None, None),
            P(("station", "group")),
            P(("station", "group"), "bias", None),
            P("bias", "station", None),
            P(("station", "group"), None),
        ),
        out_specs=(P("bias", "station", None, None), P(("station", "group"), None)),
        check_vma=False,
    )
```

time: 213 us -> 90.5 us (0.42); the launches traced: 209 us -> 90.3 us
  other arithmetic: 89.1 us -> 0 us
  Pallas kernels: 0 us -> 84 us
  blocking collectives: 59.7 us -> 0 us
  waiting for transfers between devices: 26.2 us -> 0 us
  matrix products: 24.8 us -> 0 us
  starting transfers between devices: 3.87 us -> 0 us
    another operation x12 -> x0, other arithmetic: 87.8 us -> none  [the longest x7 47.7 us: spd_inverse(): factor = jnp.linalg.cholesky(matrix)]
    pallas_call x0 -> x3, Pallas kernels: none -> 84 us  [the longest x1 65.1 us: local(): pl.pallas_call(k2_body, out_shape=(jax.ShapeDtypeStruct((BS, BS), F32), j...]
    all_to_all x2 -> x0, blocking collectives: 55.9 us -> none  [the longest x1 39.9 us: summed_on_arrival(): lax.all_to_all(blocks, axis, split_axis=0, concat_axis=0, tiled=True)]
    all_to_all x1 -> x0, waiting for transfers between devices: 26.2 us -> none  [from_everyone(): return lax.all_to_all(copies, axis, split_axis=0, concat_axis=0, tiled=True)]
    dot_general x10 -> x0, matrix products: 24.1 us -> none  [the longest x1 6.9 us: local(): jnp.einsum('shjac,shjad->shjcd', weighted, weighted - solved, precision=p...]
    unnamed x10 -> x14, local copies, waits for them, and re-layouts: 0.03 us -> 5.54 us
    all_gather x1 -> x0, blocking collectives: 3.88 us -> none  [gathered_total(): blocks = lax.all_gather(value, axis)]
    all_to_all x1 -> x0, starting transfers between devices: 3.87 us -> none  [from_everyone(): return lax.all_to_all(copies, axis, split_axis=0, concat_axis=0, tiled=True)]
  transfers between devices with their start and end apart: 1 -> 0, of which waited for: 1 -> 0; matrix products, arithmetic and copies ran while one was open for 0% -> 0% of each run, Pallas kernels for 0% -> 0%
where the time goes in v1:
time: 90.5 us; the launch traced here: 90.3 us
  Pallas kernels  84 us (93%)
  local copies, waits for them, and re-layouts  5.54 us (6%)
    pallas_call x1, Pallas kernels, local(): pl.pallas_call(k2_body, out_shape=(jax.ShapeDtypeStruct((BS, BS), F32), j...  65.1 us
    pallas_call x1, Pallas kernels, local(): pl.pallas_call(lambda l, v, n, c, t, s, i, slot, b, w2, v2: k1_body(l, v,...  10.4 us
    pallas_call x1, Pallas kernels, local(): pl.pallas_call(k3_body, out_shape=jax.ShapeDtypeStruct((S, A * A), F32),...  8.54 us
    unnamed x14, local copies, waits for them, and re-layouts  5.54 us

profile of v1, /device:TPU:1, one launch (start us, length us, event | category | flops | bytes accessed | tf_op | source)
XLA Modules:
  0.0 90.3 jit_solution(18102828222916824177)
XLA Ops:
  0.6 0.0 copy-start
  0.6 1.4 %copy-done = f32[8,1,8,48,128]{4,3,2,1,0:T(8,128)S(1)} copy-done((f32[8,1,8,48,128]{4,3,2,1,0:T(8,128)S(1)}, f32[8,1,8,48,128]{4,3,2,1,0:T(8,128)}, u32[]{:S(2)}) %copy-start) | copy-done | bytes 1572888
  2.0 0.0 copy-start.1
  2.0 0.9 copy-done.1
  2.9 0.0 copy-start.3
  2.9 0.7 copy-done.3
  3.6 0.0 copy-start.4
  3.6 0.7 copy-done.4
  4.3 0.0 copy-start.2
  4.3 10.4 %local_terms.1 = (f32[8,16,16,128]{3,2,1,0:T(8,128)S(1)}, bf16[8,9,48,256]{3,2,1,0:T(8,128)(2,1)S(1)}, f32[8,48,48]{2,1,0:T(8,128)S(1)}, s32[8,17]{1,0:T(8,128)S(1)}) custom-call(s32[8]{0:T(128)S(1)} %copy-done.4, s32[8,8]{1,0:T(8,128)S(1)} %bitcast.6, f32[8,2304]{1,0:T(8,128)S(1)} %copy-done.1, f32[8,8,48,128]{3,2,1,0:T(8,128)S(1)} %bitcast.4), custom_call_target="tpu_custom_call" | custom-call | tf_op jit(solution)/shard_map/local_terms/pallas_call | solution.py:350
  14.6 0.0 copy-start.5
  14.6 0.6 copy-done.5
  15.3 65.1 %block_cov.1 = (f32[128,128]{1,0:T(8,128)S(1)}, f32[8,16,16,128]{3,2,1,0:T(8,128)S(1)}) custom-call(f32[8,16,16,128]{3,2,1,0:T(8,128)S(1)} %get-tuple-element.8.table_ref, f32[1,128]{1,0:T(1,128)S(1)} %bitcast.8), custom_call_target="tpu_custom_call" | custom-call | tf_op jit(solution)/shard_map/block_cov/pallas_call | solution.py:369
  80.4 0.0 copy-done.2
  80.4 8.5 %amb_cov.1 = f32[8,2304]{1,0:T(8,128)S(1)} custom-call(s32[8]{0:T(128)S(1)} %copy-done.4, s32[8,8]{1,0:T(8,128)S(1)} %bitcast.7, s32[8,17]{1,0:T(8,128)S(1)} %get-tuple-element.10.slot_ref, bf16[8,9,48,256]{3,2,1,0:T(8,128)(2,1)S(1)} %get-tuple-element.11.s_ref, f32[8,16,16,128]{3,2,1,0:T(8,128)S(1)} %get-tuple-element.12.call_ref, ...), custom_call_target="tpu_custom_call" | custom-call | tf_op jit(solution)/shard_map/amb_cov/pallas_call | solution.py:390
  89.0 0.6 copy.10
  89.6 0.6 copy.11
Async XLA Ops:
  0.6 1.4 %copy-start = (f32[8,1,8,48,128]{4,3,2,1,0:T(8,128)S(1)}, f32[8,1,8,48,128]{4,3,2,1,0:T(8,128)}, u32[]{:S(2)}) copy-start(f32[8,1,8,48,128]{4,3,2,1,0:T(8,128)} %param.7) | copy-start | bytes 4718596
  2.0 0.9 copy-start.1
  2.9 0.7 copy-start.3
  3.6 0.7 copy-start.4
  4.3 76.2 %copy-start.2 = (s32[8,2304]{1,0:T(8,128)S(1)}, s32[8,2304]{1,0:T(8,128)}, u32[]{:S(2)}) copy-start(s32[8,2304]{1,0:T(8,128)} %um_ref.1) | copy-start | bytes 221188
  14.6 0.7 copy-start.5

commit v2 on v1

v2 whole, which is shorter than its diff:
```python
import jax
import jax.numpy as jnp
from jax import lax
from jax.experimental import pallas as pl
from jax.experimental.pallas import tpu as pltpu
from jax.sharding import PartitionSpec as P

A = 48
BS = 128
VH = 8
S = 8
NH = 16
NST = 16
NG = 8
HALF = A // 2
MESH = pl.DeviceIdType.MESH
F32 = jnp.float32
BF16 = jnp.bfloat16
I32 = jnp.int32
VMEM_LIMIT = 48 * 1024 * 1024


def lanes_of(shape=(8, 128)):
    return lax.broadcasted_iota(I32, shape, 1)


def subs_of(shape=(8, 128)):
    return lax.broadcasted_iota(I32, shape, 0)


def pick(x, idx):
    return jnp.take_along_axis(x, idx, axis=1, mode="promise_in_bounds")


def split2(x):
    hi = x.astype(BF16)
    lo = (x - hi.astype(F32)).astype(BF16)
    return hi, lo


def inv2(m):
    (a, b), (c, d) = m
    r = 1.0 / (a * d - b * c)
    return [[d * r, -(b * r)], [-(c * r), a * r]]


def mul2(m, n):
    return [[m[i][0] * n[0][j] + m[i][1] * n[1][j] for j in range(2)] for i in range(2)]


def inv4(p):
    a = [[p[i][j] for j in range(2)] for i in range(2)]
    b = [[p[i][j + 2] for j in range(2)] for i in range(2)]
    c = [[p[i + 2][j] for j in range(2)] for i in range(2)]
    d = [[p[i + 2][j + 2] for j in range(2)] for i in range(2)]
    ai = inv2(a)
    t = mul2(ai, b)
    u = mul2(c, ai)
    ct = mul2(c, t)
    si = inv2([[d[i][j] - ct[i][j] for j in range(2)] for i in range(2)])
    ts = mul2(t, si)
    su = mul2(si, u)
    tsu = mul2(ts, u)
    out = [[None] * 4 for _ in range(4)]
    for i in range(2):
        for j in range(2):
            out[i][j] = ai[i][j] + tsu[i][j]
            out[i][j + 2] = -ts[i][j]
            out[i + 2][j] = -su[i][j]
            out[i + 2][j + 2] = si[i][j]
    return out


def scaled_rows(pinv, rows, col, k):
    inside = (col >= k) & (col < k + 4)
    rows = [jnp.where(inside, (col == k + q).astype(F32), rows[q]) for q in range(4)]
    out = []
    for q in range(4):
        out.append((pinv[q][0] * rows[0] + pinv[q][1] * rows[1]) + (pinv[q][2] * rows[2] + pinv[q][3] * rows[3]))
    return inside, out


def unpack_rows(ref, base):
    lane = lanes_of()
    vregs = [ref[:, 128 * v : 128 * (v + 1)] for v in range(18)]
    out = []
    for r in range(HALF):
        v, o = divmod(A * r, 128)

        def part(first, shift):
            head = vregs[first] if shift == 0 else pltpu.roll(vregs[first], shift, 1)
            return head

        low = part(v, (128 - o) % 128)
        high = part(v + 9, (192 - o) % 128)
        if o + A > 128:
            low = jnp.where(lane < 128 - o, low, part(v + 1, (128 - o) % 128))
            high = jnp.where(lane < 192 - o, high, part(v + 10, (192 - o) % 128))
        out.append(jnp.where(lane < 64, low, high))
    return out


def len_column(len_ref):
    sub = subs_of()
    out = jnp.zeros((8, 128), I32)
    for s in range(S):
        out = jnp.where(sub == s, len_ref[s], out)
    return out


def invert48(rows, lens):
    lane = lanes_of()
    col = lane & 63
    side = lane & 64
    m = []
    for r in range(HALF):
        row_id = jnp.where(lane < 64, r, r + HALF)
        m.append(jnp.where((row_id < lens) & (col < lens), rows[r], (col == row_id).astype(F32)))
    for k in range(0, A, 4):
        high = k >= HALF
        r0 = k % HALF
        base = 64 if high else 0
        dup = col + base
        piv = [m[r0 + q] for q in range(4)]
        p = [[pick(piv[q], jnp.full((8, 128), base + k + r, I32)) for r in range(4)] for q in range(4)]
        pinv = inv4(p)
        inside, rh = scaled_rows(pinv, [pick(piv[q], dup) for q in range(4)], col, k)
        idx = [side + (k + q) for q in range(4)]
        own_half = (lane >= 64) if high else (lane < 64)
        new = []
        for r in range(HALF):
            c = [pick(m[r], idx[q]) for q in range(4)]
            upd = (c[0] * rh[0] + c[1] * rh[1]) + (c[2] * rh[2] + c[3] * rh[3])
            v = jnp.where(inside, 0.0, m[r]) - upd
            if r0 <= r < r0 + 4:
                v = jnp.where(own_half, rh[r - r0], v)
            new.append(v)
        m = new
    return m


def to_stations(m, buf):
    for r in range(HALF):
        buf[8 * r : 8 * r + 8, :] = m[r]
        buf[8 * (r + HALF) : 8 * (r + HALF) + 8, :] = pltpu.roll(m[r], 64, 1)


def station(buf, s):
    return buf[pl.ds(s, A, stride=S), :][:, :A]


def invert128(mat):
    lane = lanes_of()
    sub = subs_of()
    m = list(mat)
    for k in range(0, BS, 4):
        t, o = divmod(k, 8)
        rows = [jnp.broadcast_to(m[t][o + q : o + q + 1, :], (8, 128)) for q in range(4)]
        at = [jnp.full((8, 128), k + q, I32) for q in range(4)]
        p = [[pick(rows[q], at[r]) for r in range(4)] for q in range(4)]
        inside, rh = scaled_rows(inv4(p), rows, lane, k)
        new = []
        for i in range(16):
            c = [pick(m[i], at[q]) for q in range(4)]
            upd = (c[0] * rh[0] + c[1] * rh[1]) + (c[2] * rh[2] + c[3] * rh[3])
            v = jnp.where(inside, 0.0, m[i]) - upd
            if i == t:
                for q in range(4):
                    v = jnp.where(sub == o + q, rh[q], v)
            new.append(v)
        m = new
    return m


def peer(axis, index):
    return {axis: index}


CH = 4
XC = NH // CH


def body(len_ref, vis_ref, prior_ref, nm_hbm, cp_hbm, um_hbm, cov_ref, amb_ref,
         nm, cp, um, buf, w2, v2, s2, slot, invs, table, r1, part, r2, piece, blk, seg, own, call, sx, lx, mine, theirs,
         loc, s1, q1, s2s, q2, s3, q3, s4, q4, s5, q5, s6, q6):
    me_g = lax.axis_index("group")
    me_s = lax.axis_index("station")
    me_b = lax.axis_index("bias")
    gp = [lax.rem(me_g + d, NG) for d in (1, 7, 2, 6, 3, 5, 4)]
    sp = [lax.rem(me_s + d, NST) for d in (8, 9, 7, 6, 10, 5, 11, 4, 12, 3, 13, 2, 14, 1, 15)]
    nm_copy = pltpu.make_async_copy(nm_hbm, nm, loc.at[0])
    nm_copy.start()
    cp_copy = [pltpu.make_async_copy(cp_hbm.at[s], cp.at[s], loc.at[2 + s]) for s in range(S)]
    for c in cp_copy:
        c.start()
    um_copy = pltpu.make_async_copy(um_hbm, um, loc.at[1])
    um_copy.start()
    barrier = pltpu.get_barrier_semaphore()
    for g in gp:
        pl.semaphore_signal(barrier, inc=1, device_id=peer("group", g), device_id_type=MESH)
    for s in sp:
        pl.semaphore_signal(barrier, inc=1, device_id=peer("station", s), device_id_type=MESH)
    pl.semaphore_signal(barrier, inc=1, device_id=peer("bias", 1 - me_b), device_id_type=MESH)

    def remote(src, dst, ss, rs, axis, index):
        return pltpu.make_async_remote_copy(src_ref=src, dst_ref=dst, send_sem=ss, recv_sem=rs, device_id=peer(axis, index), device_id_type=MESH)

    sent = []

    def send(*args):
        copy = remote(*args)
        copy.start()
        sent.append(copy)

    def arrived(*args):
        remote(*args).wait_recv()

    lens = len_column(len_ref)
    nm_copy.wait()
    to_stations(invert48(unpack_rows(nm, 0), lens), buf)
    zeros = jnp.zeros((A, 2 * BS), BF16)
    for s in range(S):
        inv = station(buf, s)
        invs[s] = inv
        lhs = jnp.concatenate(split2(inv), axis=0)
        keep = lax.broadcasted_iota(I32, (A, BS), 0) < len_ref[s]
        cp_copy[s].wait()
        for j in range(VH):
            w = jnp.where(keep, cp[s, j], 0.0)
            wp = jnp.concatenate(split2(w), axis=1)
            w2[s, j] = wp
            out = jnp.dot(lhs, wp, preferred_element_type=F32)
            out = out[:A] + out[A:]
            sol = out[:, :BS] + out[:, BS:]
            s2[s, j] = jnp.concatenate(split2(sol), axis=1)
            v2[s, j] = jnp.concatenate(split2(w - sol), axis=1)
        w2[s, VH] = zeros
        v2[s, VH] = zeros
        s2[s, VH] = zeros

    for ch in range(CH):
        for x in range(XC * ch, XC * ch + XC):
            at = []
            for s in range(S):
                j = jnp.int32(VH)
                for jj in range(VH):
                    j = jnp.where(vis_ref[s, jj] == x, jj, j)
                slot[s, x] = j
                at.append(j)
            wx = jnp.concatenate([w2[s, at[s]] for s in range(S)], axis=0)
            vx = jnp.concatenate([v2[s, at[s]] for s in range(S)], axis=0)
            out = lax.dot_general(wx, vx, (((0,), (0,)), ((), ())), preferred_element_type=F32)
            out = out[:BS] + out[BS:]
            out = out[:, :BS] + out[:, BS:]
            for g in range(NG):
                table[g, x] = out[16 * g : 16 * g + 16]
        if ch == 0:
            pl.semaphore_wait(barrier, NG - 1 + NST - 1 + 1)
        xs = pl.ds(XC * ch, XC)
        for g in gp:
            send(table.at[g, xs], r1.at[me_g, xs], s1.at[ch, g], q1.at[ch, me_g], "group", g)
    for ch in range(CH):
        xs = pl.ds(XC * ch, XC)
        total = table[me_g, xs]
        for g in gp:
            arrived(table.at[g, xs], r1.at[g, xs], s1.at[ch, g], q1.at[ch, g], "group", g)
        for g in gp:
            total = total + r1[g, xs]
        part[xs] = total
    for s in sp:
        send(part.at[s], r2.at[me_s], s2s.at[s], q2.at[me_s], "station", s)
    total = part[me_s]
    for s in sp:
        arrived(part.at[s], r2.at[s], s2s.at[s], q2.at[s], "station", s)
    for s in sp:
        total = total + r2[s]
    piece[...] = total
    for g in gp:
        send(piece, blk.at[me_g], s3.at[g], q3.at[me_g], "group", g)
    blk[me_g] = total
    for g in gp:
        arrived(piece, blk.at[g], s3.at[g], q3.at[g], "group", g)
    lane = lanes_of()
    sub = subs_of()
    prior = jnp.broadcast_to(prior_ref[...], (8, 128))
    mat = []
    for i in range(16):
        tile = blk[i // 2, 8 * (i % 2) : 8 * (i % 2) + 8, :]
        mat.append(tile + jnp.where(lane == sub + 8 * i, prior, 0.0))
    mat = invert128(mat)
    for i in range(16):
        own[i // 2, 8 * (i % 2) : 8 * (i % 2) + 8, :] = mat[i]
        cov_ref[8 * i : 8 * i + 8, :] = mat[i]
    for s in sp:
        send(own.at[me_g], seg.at[me_s], s4.at[s], q4.at[me_s], "station", s)
    seg[me_s] = own[me_g]
    um_copy.wait()
    to_stations([z.astype(F32) for z in unpack_rows(um, 0)], buf)
    zs = [station(buf, s).astype(BF16) for s in range(S)]
    for s in sp:
        arrived(own.at[me_g], seg.at[s], s4.at[s], q4.at[s], "station", s)
    for ch in range(CH):
        xs = pl.ds(XC * ch, XC)
        for g in gp:
            send(seg.at[xs], call.at[me_g, xs], s5.at[ch, g], q5.at[ch, me_g], "group", g)
    call[me_g] = seg[...]
    for ch in range(CH):
        xs = pl.ds(XC * ch, XC)
        for g in gp:
            arrived(seg.at[xs], call.at[g, xs], s5.at[ch, g], q5.at[ch, g], "group", g)
        for x in range(XC * ch, XC * ch + XC):
            sg = [s2[s, slot[s, x]] for s in range(S)]
            c = jnp.concatenate([call[g, x] for g in range(NG)], axis=0)
            c2 = jnp.concatenate(split2(c), axis=1)
            c4 = jnp.concatenate([c2, c2], axis=0)
            out = jnp.dot(jnp.concatenate(sg, axis=0), c4, preferred_element_type=F32)
            hi, lo = split2(out[:, :BS] + out[:, BS:])
            at = slice(BS * x, BS * x + BS)
            for s in range(S):
                sx[s, :A, at] = sg[s][:, :BS]
                sx[s, A:, at] = sg[s][:, BS:]
                lx[s, :A, at] = hi[A * s : A * s + A]
                lx[s, A:, at] = lo[A * s : A * s + A]
    nt = (((1,), (1,)), ((), ()))
    for s in range(S):
        out = lax.dot_general(lx[s], sx[s], nt, preferred_element_type=F32)
        out = out[:A] + out[A:]
        mine[s] = out[:, :A] + out[:, A:]
    send(mine, theirs, s6, q6, "bias", 1 - me_b)
    arrived(mine, theirs, s6, q6, "bias", 1 - me_b)
    ri = lax.broadcasted_iota(I32, (A, A), 0)
    ci = lax.broadcasted_iota(I32, (A, A), 1)
    for s in range(S):
        keep = (ri < len_ref[s]) & (ci < len_ref[s])
        cov = jnp.where(keep, invs[s] + (mine[s] + theirs[s]), 0.0)
        hi, lo = split2(cov)
        t = jnp.dot(zs[s], hi, preferred_element_type=F32) + jnp.dot(zs[s], lo, preferred_element_type=F32)
        hi, lo = split2(t)
        o = lax.dot_general(hi, zs[s], nt, preferred_element_type=F32) + lax.dot_general(lo, zs[s], nt, preferred_element_type=F32)
        o = jnp.where(keep, o, 0.0)
        buf[pl.ds(s, A, stride=S), :] = jnp.concatenate([o, jnp.zeros((A, 128 - A), F32)], axis=1)
    acc = [None] * 18
    for i in range(A):
        v, o = divmod(A * i, 128)
        row = buf[8 * i : 8 * i + 8, :]
        row = pltpu.roll(row, o, 1) if o else row
        acc[v] = row if acc[v] is None else jnp.where(lane >= o, row, acc[v])
        if o + A > 128:
            acc[v + 1] = row
    for v in range(18):
        amb_ref[:, 128 * v : 128 * v + 128] = acc[v]
    for copy in sent:
        copy.wait_send()


def local(normal_mat, coupling, lengths, visible, bias_prior, unimod):
    vm = pl.BlockSpec(memory_space=pltpu.VMEM)
    sm = pl.BlockSpec(memory_space=pltpu.SMEM)
    hb = pl.BlockSpec(memory_space=pltpu.HBM)
    dma = pltpu.SemaphoreType.DMA
    vmem = pltpu.VMEM
    slots = vmem((S, VH + 1, A, 2 * BS), BF16)
    wide = vmem((S, 2 * A, NH * BS), BF16)
    full = vmem((NG, NH, 16, BS), F32)
    row = vmem((NH, 16, BS), F32)
    cov, amb = pl.pallas_call(
        body,
        out_shape=(jax.ShapeDtypeStruct((BS, BS), F32), jax.ShapeDtypeStruct((S, A * A), F32)),
        in_specs=[sm, sm, vm, hb, hb, hb],
        out_specs=(vm, vm),
        scratch_shapes=[
            vmem((S, A * A), F32),
            vmem((S, VH, A, BS), F32),
            vmem((S, A * A), I32),
            vmem((A * S, 128), F32),
            slots, slots, slots,
            pltpu.SMEM((S, NH), I32),
            vmem((S, A, A), F32),
            full, full,
            row, row,
            vmem((16, BS), F32),
            vmem((NG, 16, BS), F32),
            row,
            vmem((NG, 16, BS), F32),
            full,
            wide, wide,
            vmem((S, A, A), F32), vmem((S, A, A), F32),
            dma((2 + S,)),
            dma((CH, NG)), dma((CH, NG)), dma((NST,)), dma((NST,)), dma((NG,)), dma((NG,)),
            dma((NST,)), dma((NST,)), dma((CH, NG)), dma((CH, NG)), dma(()), dma(()),
        ],
        compiler_params=pltpu.CompilerParams(vmem_limit_bytes=VMEM_LIMIT, collective_id=0, has_side_effects=True),
        name="epoch",
    )(
        lengths,
        visible.reshape(S, VH),
        bias_prior.reshape(1, BS),
        normal_mat,
        coupling.reshape(S, VH, A, BS),
        unimod,
    )
    return (cov.reshape(1, 1, BS, BS), amb)


def solution(mesh):
    return jax.shard_map(
        local,
        mesh=mesh,
        in_specs=(
            P(("station", "group"), None),
            P(("station", "group"), "bias", None, None, None),
            P(("station", "group")),
            P(("station", "group"), "bias", None),
            P("bias", "station", None),
            P(("station", "group"), None),
        ),
        out_specs=(P("bias", "station", None, None), P(("station", "group"), None)),
        check_vma=False,
    )
```

time: 90.5 us -> 80.1 us (0.89)
  Pallas kernels: 84 us -> 72.8 us
    pallas_call x3 -> x1, Pallas kernels: 84 us -> 72.8 us  [local(): pl.pallas_call(body, out_shape=(jax.ShapeDtypeStruct((BS, BS), F32), jax....]
where the time goes in v2:
time: 80.1 us; the launch traced here: 79.9 us
  Pallas kernels  72.8 us (91%)
  local copies, waits for them, and re-layouts  6.43 us (8%)
    pallas_call x1, Pallas kernels, local(): pl.pallas_call(body, out_shape=(jax.ShapeDtypeStruct((BS, BS), F32), jax....  72.8 us
    unnamed x14, local copies, waits for them, and re-layouts  6.43 us

profile of v2, /device:TPU:1, one launch (start us, length us, event | category | flops | bytes accessed | tf_op | source)
XLA Modules:
  0.0 79.9 jit_solution(8188015959634905125)
XLA Ops:
  0.6 0.0 copy-start
  0.6 1.4 %copy-done = f32[8,1,8,48,128]{4,3,2,1,0:T(8,128)S(1)} copy-done((f32[8,1,8,48,128]{4,3,2,1,0:T(8,128)S(1)}, f32[8,1,8,48,128]{4,3,2,1,0:T(8,128)}, u32[]{:S(2)}) %copy-start) | copy-done | bytes 1572888
  2.0 0.0 copy-start.1
  2.0 0.9 %copy-done.1 = f32[8,2304]{1,0:T(8,128)S(1)} copy-done((f32[8,2304]{1,0:T(8,128)S(1)}, f32[8,2304]{1,0:T(8,128)}, u32[]{:S(2)}) %copy-start.1) | copy-done | bytes 73752
  2.9 0.0 copy-start.2
  2.9 0.9 %copy-done.2 = s32[8,2304]{1,0:T(8,128)S(1)} copy-done((s32[8,2304]{1,0:T(8,128)S(1)}, s32[8,2304]{1,0:T(8,128)}, u32[]{:S(2)}) %copy-start.2) | copy-done | bytes 73752
  3.8 0.0 copy-start.3
  3.8 0.7 copy-done.3
  4.5 0.0 copy-start.4
  4.5 0.7 copy-done.4
  5.2 0.0 copy-start.5
  5.2 0.7 copy-done.5
  5.8 72.8 %epoch.1 = (f32[128,128]{1,0:T(8,128)S(1)}, f32[8,2304]{1,0:T(8,128)S(1)}) custom-call(s32[8]{0:T(128)S(1)} %copy-done.4, s32[8,8]{1,0:T(8,128)S(1)} %bitcast.6, f32[1,128]{1,0:T(1,128)S(1)} %bitcast.7, f32[8,2304]{1,0:T(8,128)S(1)} %copy-done.1, f32[8,8,48,128]{3,2,1,0:T(8,128)S(1)} %bitcast.4, s32[8,2304]{1,0:T(8,128)S(1)} %copy-done.2), custom_call_target="tpu_custom_call" | custom-call | tf_op jit(solution)/shard_map/epoch/pallas_call | solution.py:366
  78.6 0.6 copy.10
  79.3 0.6 copy.11
Async XLA Ops:
  0.6 1.4 %copy-start = (f32[8,1,8,48,128]{4,3,2,1,0:T(8,128)S(1)}, f32[8,1,8,48,128]{4,3,2,1,0:T(8,128)}, u32[]{:S(2)}) copy-start(f32[8,1,8,48,128]{4,3,2,1,0:T(8,128)} %param.7) | copy-start | bytes 4718596
  2.0 0.9 %copy-start.1 = (f32[8,2304]{1,0:T(8,128)S(1)}, f32[8,2304]{1,0:T(8,128)}, u32[]{:S(2)}) copy-start(f32[8,2304]{1,0:T(8,128)} %nm_hbm.1) | copy-start | bytes 221188
  2.9 0.9 %copy-start.2 = (s32[8,2304]{1,0:T(8,128)S(1)}, s32[8,2304]{1,0:T(8,128)}, u32[]{:S(2)}) copy-start(s32[8,2304]{1,0:T(8,128)} %um_hbm.1) | copy-start | bytes 221188
  3.8 0.7 copy-start.3
  4.5 0.7 copy-start.4
  5.2 0.7 copy-start.5

commit v3 on v2

--- a/solution.py
+++ b/solution.py
@@ -17,7 +17,7 @@
 F32 = jnp.float32
 BF16 = jnp.bfloat16
 I32 = jnp.int32
-VMEM_LIMIT = 48 * 1024 * 1024
+VMEM_LIMIT = 63 * 1024 * 1024
 
 
 def lanes_of(shape=(8, 128)):
@@ -178,15 +178,42 @@
 
 CH = 4
 XC = NH // CH
+HB = BS // 2
+
+
+def pack_half(top, bot):
+    row = lax.broadcasted_iota(I32, (HB, BS), 0)
+    lane = lax.broadcasted_iota(I32, (HB, BS), 1)
+    return jnp.where((lane >= HB) | (row > lane), top, pltpu.roll(bot, HB, 1))
+
+
+def diag_tile(top):
+    lane = lanes_of()
+    sub = subs_of()
+    out = jnp.zeros((8, BS), F32)
+    for t in range(8):
+        out = jnp.where(lane == sub + 8 * t, top[8 * t : 8 * t + 8], out)
+    return out
+
+
+def unpack_half(p, e):
+    row = lax.broadcasted_iota(I32, (HB, BS), 0)
+    lane = lax.broadcasted_iota(I32, (HB, BS), 1)
+    t = jnp.concatenate([p, jnp.zeros((HB, BS), F32)], axis=0).T
+    e = jnp.concatenate([e] * 8, axis=0)
+    top = jnp.where((lane >= HB) | (row > lane), p, jnp.where(row == lane, e, t[:HB]))
+    low = pltpu.roll(jnp.where(row <= lane, p, t[:HB]), HB, 1)
+    return jnp.concatenate([top, jnp.where(lane < HB, t[HB:], low)], axis=0)
 
 
 def body(len_ref, vis_ref, prior_ref, nm_hbm, cp_hbm, um_hbm, cov_ref, amb_ref,
-         nm, cp, um, buf, w2, v2, s2, slot, invs, table, r1, part, r2, piece, blk, seg, own, call, sx, lx, mine, theirs,
-         loc, s1, q1, s2s, q2, s3, q3, s4, q4, s5, q5, s6, q6):
+         nm, cp, um, buf, w2, v2, s2, slot, invs, table, ediag, r1, part, r2, rd2, piece, blk, eblk, own, seg, call, dall,
+         sx, lx, mine, theirs,
+         loc, s1, q1, s2s, q2, d2s, d2q, s3, q3, d3s, d3q, s4, q4, d4s, d4q, s5, q5, d5s, d5q, s6, q6):
     me_g = lax.axis_index("group")
     me_s = lax.axis_index("station")
     me_b = lax.axis_index("bias")
-    gp = [lax.rem(me_g + d, NG) for d in (1, 7, 2, 6, 3, 5, 4)]
+    gp = [lax.rem(me_g + d, NG) for d in (4, 3, 5, 2, 6, 1, 7)]
     sp = [lax.rem(me_s + d, NST) for d in (8, 9, 7, 6, 10, 5, 11, 4, 12, 3, 13, 2, 14, 1, 15)]
     nm_copy = pltpu.make_async_copy(nm_hbm, nm, loc.at[0])
     nm_copy.start()
@@ -196,10 +223,10 @@
     um_copy = pltpu.make_async_copy(um_hbm, um, loc.at[1])
     um_copy.start()
     barrier = pltpu.get_barrier_semaphore()
+    for s in sp:
+        pl.semaphore_signal(barrier, inc=1, device_id=peer("station", s), device_id_type=MESH)
     for g in gp:
         pl.semaphore_signal(barrier, inc=1, device_id=peer("group", g), device_id_type=MESH)
-    for s in sp:
-        pl.semaphore_signal(barrier, inc=1, device_id=peer("station", s), device_id_type=MESH)
     pl.semaphore_signal(barrier, inc=1, device_id=peer("bias", 1 - me_b), device_id_type=MESH)
 
     def remote(src, dst, ss, rs, axis, index):
@@ -214,6 +241,13 @@
 
     def arrived(*args):
         remote(*args).wait_recv()
+
+    lane = lanes_of()
+    sub = subs_of()
+    near = XC * (me_s // XC)
+    far_first = [lax.rem(near + XC * d, NH) for d in (2, 1, 3, 0)]
+    near_first = [lax.rem(near + XC * d, NH) for d in (0, 1, 3, 2)]
+    diag_owner = me_g == me_s // 2
 
     lens = len_column(len_ref)
     nm_copy.wait()
@@ -238,8 +272,9 @@
         v2[s, VH] = zeros
         s2[s, VH] = zeros
 
-    for ch in range(CH):
-        for x in range(XC * ch, XC * ch + XC):
+    for i, x0 in enumerate(far_first):
+        for dx in range(XC):
+            x = x0 + dx
             at = []
             for s in range(S):
                 j = jnp.int32(VH)
@@ -252,87 +287,181 @@
             out = lax.dot_general(wx, vx, (((0,), (0,)), ((), ())), preferred_element_type=F32)
             out = out[:BS] + out[BS:]
             out = out[:, :BS] + out[:, BS:]
+            packed = pack_half(out[:HB], out[HB:])
             for g in range(NG):
-                table[g, x] = out[16 * g : 16 * g + 16]
-        if ch == 0:
+                table[g, x] = packed[8 * g : 8 * g + 8]
+            ediag[x] = diag_tile(out[:HB])
+        if i == 0:
             pl.semaphore_wait(barrier, NG - 1 + NST - 1 + 1)
-        xs = pl.ds(XC * ch, XC)
         for g in gp:
-            send(table.at[g, xs], r1.at[me_g, xs], s1.at[ch, g], q1.at[ch, me_g], "group", g)
-    for ch in range(CH):
-        xs = pl.ds(XC * ch, XC)
+            send(table.at[g, pl.ds(x0, XC)], r1.at[me_g, pl.ds(x0, XC)], s1.at[i, g], q1.at[i, me_g], "group", g)
+    both = jnp.zeros((8, BS), F32)
+    for x in range(NH):
+        e = ediag[x]
+        e = pltpu.roll(e, x % 8, 0) if x % 8 else e
+        both = both + (pltpu.roll(e, HB, 1) if x >= 8 else e)
+    ediag[NH] = both
+    for g in gp:
+        send(ediag.at[NH], r1.at[me_g, NH], s1.at[CH, g], q1.at[CH, me_g], "group", g)
+
+    def to_owner(x):
+        return remote(part.at[x], r2.at[me_s], s2s.at[x], q2.at[me_s], "station", x)
+
+    for i, x0 in enumerate(far_first):
+        xs = pl.ds(x0, XC)
         total = table[me_g, xs]
         for g in gp:
-            arrived(table.at[g, xs], r1.at[g, xs], s1.at[ch, g], q1.at[ch, g], "group", g)
-        for g in gp:
+            arrived(table.at[g, xs], r1.at[g, xs], s1.at[i, g], q1.at[i, g], "group", g)
             total = total + r1[g, xs]
         part[xs] = total
-    for s in sp:
-        send(part.at[s], r2.at[me_s], s2s.at[s], q2.at[me_s], "station", s)
+        for dx in range(XC):
+            x = x0 + dx
+
+            @pl.when(x != me_s)
+            def _():
+                to_owner(x).start()
+
+    total = both
+    for g in gp:
+        arrived(ediag.at[NH], r1.at[g, NH], s1.at[CH, g], q1.at[CH, g], "group", g)
+        total = total + r1[g, NH]
+    part[NH] = total
+
+    def diag_to_owner(h):
+        return remote(part.at[NH], rd2.at[me_s], d2s.at[h], d2q.at[me_s], "station", 2 * me_g + h)
+
+    for h in range(2):
+
+        @pl.when(2 * me_g + h != me_s)
+        def _():
+            diag_to_owner(h).start()
+
     total = part[me_s]
-    for s in sp:
+    for s in sp[::-1]:
         arrived(part.at[s], r2.at[s], s2s.at[s], q2.at[s], "station", s)
-    for s in sp:
         total = total + r2[s]
     piece[...] = total
     for g in gp:
         send(piece, blk.at[me_g], s3.at[g], q3.at[me_g], "group", g)
     blk[me_g] = total
+
+    def diag_to_peer(g):
+        return remote(piece_e, eblk, d3s.at[g], d3q.at[0], "group", g)
+
+    piece_e = part.at[NH + 1]
+
+    @pl.when(diag_owner)
+    def _():
+        e = part[NH]
+        for s in sp:
+            arrived(part.at[NH], rd2.at[s], d2s.at[0], d2q.at[s], "station", s)
+            e = e + rd2[s]
+        e = pltpu.roll(e, lax.rem(8 - lax.rem(me_s, 8), 8), 0)
+        e = pltpu.roll(e, HB * (me_s // 8), 1)
+        part[NH + 1] = e
+        for g in gp:
+            diag_to_peer(g).start()
+        eblk[...] = e
+
     for g in gp:
         arrived(piece, blk.at[g], s3.at[g], q3.at[g], "group", g)
-    lane = lanes_of()
-    sub = subs_of()
+
+    @pl.when(me_g != me_s // 2)
+    def _():
+        arrived(piece_e, eblk, d3s.at[0], d3q.at[0], "group", me_s // 2)
+
     prior = jnp.broadcast_to(prior_ref[...], (8, 128))
-    mat = []
-    for i in range(16):
-        tile = blk[i // 2, 8 * (i % 2) : 8 * (i % 2) + 8, :]
-        mat.append(tile + jnp.where(lane == sub + 8 * i, prior, 0.0))
+    full = unpack_half(jnp.concatenate([blk[g] for g in range(NG)], axis=0), eblk[...])
+    mat = [full[8 * i : 8 * i + 8] + jnp.where(lane == sub + 8 * i, prior, 0.0) for i in range(16)]
     mat = invert128(mat)
-    for i in range(16):
-        own[i // 2, 8 * (i % 2) : 8 * (i % 2) + 8, :] = mat[i]
-        cov_ref[8 * i : 8 * i + 8, :] = mat[i]
+    top = jnp.concatenate(mat[:8], axis=0)
+    packed = pack_half(top, jnp.concatenate(mat[8:], axis=0))
+    for g in range(NG):
+        own[g] = packed[8 * g : 8 * g + 8]
+    own[NG] = diag_tile(top)
     for s in sp:
         send(own.at[me_g], seg.at[me_s], s4.at[s], q4.at[me_s], "station", s)
+
+    def diag_to_station(s):
+        return remote(own.at[NG], dall.at[me_s], d4s.at[s], d4q.at[me_s], "station", s)
+
+    @pl.when(diag_owner)
+    def _():
+        for s in sp:
+            diag_to_station(s).start()
+        dall[me_s] = own[NG]
+
     seg[me_s] = own[me_g]
+    for i in range(16):
+        cov_ref[8 * i : 8 * i + 8, :] = mat[i]
     um_copy.wait()
     to_stations([z.astype(F32) for z in unpack_rows(um, 0)], buf)
     zs = [station(buf, s).astype(BF16) for s in range(S)]
-    for s in sp:
-        arrived(own.at[me_g], seg.at[s], s4.at[s], q4.at[s], "station", s)
-    for ch in range(CH):
-        xs = pl.ds(XC * ch, XC)
+    for h in range(2):
+        x = 2 * me_g + h
+
+        @pl.when(x != me_s)
+        def _():
+            arrived(own.at[NG], dall.at[x], d4s.at[0], d4q.at[x], "station", x)
+
+    pair = pl.ds(2 * me_g, 2)
+    for i, x0 in enumerate(near_first):
+        for dx in range(XC):
+            x = x0 + dx
+
+            @pl.when(x != me_s)
+            def _():
+                arrived(own.at[me_g], seg.at[x], s4.at[0], q4.at[x], "station", x)
+
+        xs = pl.ds(x0, XC)
         for g in gp:
-            send(seg.at[xs], call.at[me_g, xs], s5.at[ch, g], q5.at[ch, me_g], "group", g)
+            send(seg.at[xs], call.at[me_g, xs], s5.at[i, g], q5.at[i, me_g], "group", g)
+        if i == 0:
+            for g in gp:
+                send(dall.at[pair], dall.at[pair], d5s.at[g], d5q.at[me_g], "group", g)
     call[me_g] = seg[...]
-    for ch in range(CH):
-        xs = pl.ds(XC * ch, XC)
+    for g in gp:
+        gpair = pl.ds(2 * g, 2)
+        arrived(dall.at[gpair], dall.at[gpair], d5s.at[g], d5q.at[g], "group", g)
+    for i, x0 in enumerate(near_first):
+        xs = pl.ds(x0, XC)
         for g in gp:
-            arrived(seg.at[xs], call.at[g, xs], s5.at[ch, g], q5.at[ch, g], "group", g)
-        for x in range(XC * ch, XC * ch + XC):
+            arrived(seg.at[xs], call.at[g, xs], s5.at[i, g], q5.at[i, g], "group", g)
+        for dx in range(XC):
+            x = x0 + dx
             sg = [s2[s, slot[s, x]] for s in range(S)]
-            c = jnp.concatenate([call[g, x] for g in range(NG)], axis=0)
+            c = unpack_half(jnp.concatenate([call[g, x] for g in range(NG)], axis=0), dall[x])
             c2 = jnp.concatenate(split2(c), axis=1)
             c4 = jnp.concatenate([c2, c2], axis=0)
             out = jnp.dot(jnp.concatenate(sg, axis=0), c4, preferred_element_type=F32)
             hi, lo = split2(out[:, :BS] + out[:, BS:])
-            at = slice(BS * x, BS * x + BS)
+            n = XC * i + dx
+            at = slice(BS * n, BS * n + BS)
             for s in range(S):
                 sx[s, :A, at] = sg[s][:, :BS]
                 sx[s, A:, at] = sg[s][:, BS:]
                 lx[s, :A, at] = hi[A * s : A * s + A]
                 lx[s, A:, at] = lo[A * s : A * s + A]
     nt = (((1,), (1,)), ((), ()))
+    pad = jnp.zeros((HALF, 64 - A), F32)
     for s in range(S):
         out = lax.dot_general(lx[s], sx[s], nt, preferred_element_type=F32)
         out = out[:A] + out[A:]
-        mine[s] = out[:, :A] + out[:, A:]
-    send(mine, theirs, s6, q6, "bias", 1 - me_b)
-    arrived(mine, theirs, s6, q6, "bias", 1 - me_b)
+        out = out[:, :A] + out[:, A:]
+        mine[s] = jnp.concatenate([out[:HALF], pad, out[HALF:], pad], axis=1)
+        if s % 4 == 3:
+            ss = pl.ds(s - 3, 4)
+            send(mine.at[ss], theirs.at[ss], s6.at[s // 4], q6.at[s // 4], "bias", 1 - me_b)
     ri = lax.broadcasted_iota(I32, (A, A), 0)
     ci = lax.broadcasted_iota(I32, (A, A), 1)
     for s in range(S):
+        if s % 4 == 0:
+            ss = pl.ds(s, 4)
+            arrived(mine.at[ss], theirs.at[ss], s6.at[s // 4], q6.at[s // 4], "bias", 1 - me_b)
         keep = (ri < len_ref[s]) & (ci < len_ref[s])
-        cov = jnp.where(keep, invs[s] + (mine[s] + theirs[s]), 0.0)
+        both = mine[s] + theirs[s]
+        both = jnp.concatenate([both[:, :A], pltpu.roll(both, 64, 1)[:, :A]], axis=0)
+        cov = jnp.where(keep, invs[s] + both, 0.0)
         hi, lo = split2(cov)
         t = jnp.dot(zs[s], hi, preferred_element_type=F32) + jnp.dot(zs[s], lo, preferred_element_type=F32)
         hi, lo = split2(t)
@@ -351,6 +480,20 @@
         amb_ref[:, 128 * v : 128 * v + 128] = acc[v]
     for copy in sent:
         copy.wait_send()
+    for s in sp:
+        to_owner(s).wait_send()
+    for h in range(2):
+
+        @pl.when(2 * me_g + h != me_s)
+        def _():
+            diag_to_owner(h).wait_send()
+
+    @pl.when(diag_owner)
+    def _():
+        for g in gp:
+            diag_to_peer(g).wait_send()
+        for s in sp:
+            diag_to_station(s).wait_send()
 
 
 def local(normal_mat, coupling, lengths, visible, bias_prior, unimod):
@@ -361,8 +504,8 @@
     vmem = pltpu.VMEM
     slots = vmem((S, VH + 1, A, 2 * BS), BF16)
     wide = vmem((S, 2 * A, NH * BS), BF16)
-    full = vmem((NG, NH, 16, BS), F32)
-    row = vmem((NH, 16, BS), F32)
+    rows = vmem((NH, 8, BS), F32)
+    half = vmem((S, HALF, BS), F32)
     cov, amb = pl.pallas_call(
         body,
         out_shape=(jax.ShapeDtypeStruct((BS, BS), F32), jax.ShapeDtypeStruct((S, A * A), F32)),
@@ -376,18 +519,27 @@
             slots, slots, slots,
             pltpu.SMEM((S, NH), I32),
             vmem((S, A, A), F32),
-            full, full,
-            row, row,
-            vmem((16, BS), F32),
-            vmem((NG, 16, BS), F32),
-            row,
-            vmem((NG, 16, BS), F32),
-            full,
+            vmem((NG, NH, 8, BS), F32),
+            vmem((NH + 1, 8, BS), F32),
+            vmem((NG, NH + 1, 8, BS), F32),
+            vmem((NH + 2, 8, BS), F32),
+            rows, rows,
+            vmem((8, BS), F32),
+            vmem((NG, 8, BS), F32),
+            vmem((8, BS), F32),
+            vmem((NG + 1, 8, BS), F32),
+            rows,
+            vmem((NG, NH, 8, BS), F32),
+            rows,
             wide, wide,
-            vmem((S, A, A), F32), vmem((S, A, A), F32),
+            half, half,
             dma((2 + S,)),
-            dma((CH, NG)), dma((CH, NG)), dma((NST,)), dma((NST,)), dma((NG,)), dma((NG,)),
-            dma((NST,)), dma((NST,)), dma((CH, NG)), dma((CH, NG)), dma(()), dma(()),
+            dma((CH + 1, NG)), dma((CH + 1, NG)),
+            dma((NST,)), dma((NST,)), dma((2,)), dma((NST,)),
+            dma((NG,)), dma((NG,)), dma((NG,)), dma((1,)),
+            dma((NST,)), dma((NST,)), dma((NST,)), dma((NST,)),
+            dma((CH, NG)), dma((CH, NG)), dma((NG,)), dma((NG,)),
+            dma((2,)), dma((2,)),
         ],
         compiler_params=pltpu.CompilerParams(vmem_limit_bytes=VMEM_LIMIT, collective_id=0, has_side_effects=True),
         name="epoch",

time: 80.1 us -> 62.9 us (0.79)
  Pallas kernels: 72.8 us -> 59.1 us
  local copies, waits for them, and re-layouts: 6.43 us -> 2.99 us
    pallas_call x1, Pallas kernels: 72.8 us -> 59.1 us  [local(): pl.pallas_call(body, out_shape=(jax.ShapeDtypeStruct((BS, BS), F32), jax....]
    unnamed x14 -> x2, local copies, waits for them, and re-layouts: 6.43 us -> 2.99 us
where the time goes in v3:
time: 62.9 us; the launch traced here: 62.7 us
  Pallas kernels  59.1 us (94%)
  local copies, waits for them, and re-layouts  2.99 us (5%)
  between operations  0.64 us (1%)
    pallas_call x1, Pallas kernels, local(): pl.pallas_call(body, out_shape=(jax.ShapeDtypeStruct((BS, BS), F32), jax....  59.1 us
    unnamed x2, local copies, waits for them, and re-layouts  2.99 us

profile of v3, /device:TPU:1, one launch (start us, length us, event | category | flops | bytes accessed | tf_op | source)
XLA Modules:
  0.0 62.7 jit_solution(17316380717413064455)
XLA Ops:
  0.6 59.1 %epoch.1 = (f32[128,128]{1,0:T(8,128)}, f32[8,2304]{1,0:T(8,128)}) custom-call(s32[8]{0:T(128)} %len_ref.1, s32[8,8]{1,0:T(8,128)} %bitcast.6, f32[1,128]{1,0:T(1,128)} %bitcast.7, f32[8,2304]{1,0:T(8,128)} %nm_hbm.1, f32[8,8,48,128]{3,2,1,0:T(8,128)} %bitcast.4, s32[8,2304]{1,0:T(8,128)} %um_hbm.1), custom_call_target="tpu_custom_call" | custom-call | tf_op jit(solution)/shard_map/epoch/pallas_call | solution.py:509
  59.7 1.5 %copy.10 = f32[1,1,128,128]{3,2,1,0:T(8,128)} copy(f32[1,1,128,128]{3,2,1,0:T(8,128)} %bitcast.5) | data formatting | bytes 131072
  61.2 1.5 %copy.11 = f32[8,2304]{1,0:T(8,128)} copy(f32[8,2304]{1,0:T(8,128)} %get-tuple-element.9) | data formatting | bytes 147456

commit v4 on v3

--- a/solution.py
+++ b/solution.py
@@ -17,7 +17,7 @@
 F32 = jnp.float32
 BF16 = jnp.bfloat16
 I32 = jnp.int32
-VMEM_LIMIT = 63 * 1024 * 1024
+VMEM_LIMIT = 48 * 1024 * 1024
 
 
 def lanes_of(shape=(8, 128)):
@@ -207,14 +207,18 @@
 
 
 def body(len_ref, vis_ref, prior_ref, nm_hbm, cp_hbm, um_hbm, cov_ref, amb_ref,
-         nm, cp, um, buf, w2, v2, s2, slot, invs, table, ediag, r1, part, r2, rd2, piece, blk, eblk, own, seg, call, dall,
+         nm, cp, um, buf, w2, v2, s2, slot, invs, table, ediag, rc, tsum, r1, rd1, part, r2, rd2, piece, blk, eblk, own, seg, call, dall,
          sx, lx, mine, theirs,
-         loc, s1, q1, s2s, q2, d2s, d2q, s3, q3, d3s, d3q, s4, q4, d4s, d4q, s5, q5, d5s, d5q, s6, q6):
+         loc, sa, qa, s1, q1, d1s, d1q, s2s, q2, d2s, d2q, s3, q3, d3s, d3q, s4, q4, d4s, d4q, s5, q5, d5s, d5q, s7, q7, d7s, d7q, s6, q6):
     me_g = lax.axis_index("group")
     me_s = lax.axis_index("station")
     me_b = lax.axis_index("bias")
     gp = [lax.rem(me_g + d, NG) for d in (4, 3, 5, 2, 6, 1, 7)]
     sp = [lax.rem(me_s + d, NST) for d in (8, 9, 7, 6, 10, 5, 11, 4, 12, 3, 13, 2, 14, 1, 15)]
+    me_c = lax.rem(me_g, 2)
+    me_x = me_g // 2
+    mate = me_g + 1 - 2 * me_c
+    xp = [lax.rem(me_x + d, 4) for d in (2, 1, 3)]
     nm_copy = pltpu.make_async_copy(nm_hbm, nm, loc.at[0])
     nm_copy.start()
     cp_copy = [pltpu.make_async_copy(cp_hbm.at[s], cp.at[s], loc.at[2 + s]) for s in range(S)]
@@ -250,6 +254,7 @@
     diag_owner = me_g == me_s // 2
 
     lens = len_column(len_ref)
+
     nm_copy.wait()
     to_stations(invert48(unpack_rows(nm, 0), lens), buf)
     zeros = jnp.zeros((A, 2 * BS), BF16)
@@ -272,6 +277,13 @@
         v2[s, VH] = zeros
         s2[s, VH] = zeros
 
+    def pass_on(i):
+        xs = pl.ds(far_first[i], XC)
+        arrived(table.at[me_c, :, xs], rc.at[:, xs], sa.at[i], qa.at[i], "group", mate)
+        tsum[:, xs] = table[me_c, :, xs] + rc[:, xs]
+        for p in xp:
+            send(tsum.at[p, xs], r1.at[me_x, xs], s1.at[i, p], q1.at[i, me_x], "group", 2 * p + me_c)
+
     for i, x0 in enumerate(far_first):
         for dx in range(XC):
             x = x0 + dx
@@ -289,12 +301,14 @@
             out = out[:, :BS] + out[:, BS:]
             packed = pack_half(out[:HB], out[HB:])
             for g in range(NG):
-                table[g, x] = packed[8 * g : 8 * g + 8]
+                table[g % 2, g // 2, x] = packed[8 * g : 8 * g + 8]
             ediag[x] = diag_tile(out[:HB])
         if i == 0:
             pl.semaphore_wait(barrier, NG - 1 + NST - 1 + 1)
-        for g in gp:
-            send(table.at[g, pl.ds(x0, XC)], r1.at[me_g, pl.ds(x0, XC)], s1.at[i, g], q1.at[i, me_g], "group", g)
+        xs = pl.ds(x0, XC)
+        send(table.at[1 - me_c, :, xs], rc.at[:, xs], sa.at[i], qa.at[i], "group", mate)
+        if i > 0:
+            pass_on(i - 1)
     both = jnp.zeros((8, BS), F32)
     for x in range(NH):
         e = ediag[x]
@@ -302,17 +316,18 @@
         both = both + (pltpu.roll(e, HB, 1) if x >= 8 else e)
     ediag[NH] = both
     for g in gp:
-        send(ediag.at[NH], r1.at[me_g, NH], s1.at[CH, g], q1.at[CH, me_g], "group", g)
+        send(ediag.at[NH], rd1.at[me_g], d1s.at[g], d1q.at[me_g], "group", g)
+    pass_on(CH - 1)
 
     def to_owner(x):
         return remote(part.at[x], r2.at[me_s], s2s.at[x], q2.at[me_s], "station", x)
 
     for i, x0 in enumerate(far_first):
         xs = pl.ds(x0, XC)
-        total = table[me_g, xs]
-        for g in gp:
-            arrived(table.at[g, xs], r1.at[g, xs], s1.at[i, g], q1.at[i, g], "group", g)
-            total = total + r1[g, xs]
+        total = tsum[me_x, xs]
+        for p in xp:
+            arrived(tsum.at[p, xs], r1.at[p, xs], s1.at[i, p], q1.at[i, p], "group", 2 * p + me_c)
+            total = total + r1[p, xs]
         part[xs] = total
         for dx in range(XC):
             x = x0 + dx
@@ -323,8 +338,8 @@
 
     total = both
     for g in gp:
-        arrived(ediag.at[NH], r1.at[g, NH], s1.at[CH, g], q1.at[CH, g], "group", g)
-        total = total + r1[g, NH]
+        arrived(ediag.at[NH], rd1.at[g], d1s.at[g], d1q.at[g], "group", g)
+        total = total + rd1[g]
     part[NH] = total
 
     def diag_to_owner(h):
@@ -383,13 +398,13 @@
         send(own.at[me_g], seg.at[me_s], s4.at[s], q4.at[me_s], "station", s)
 
     def diag_to_station(s):
-        return remote(own.at[NG], dall.at[me_s], d4s.at[s], d4q.at[me_s], "station", s)
+        return remote(own.at[NG], dall.at[me_x, me_c, lax.rem(me_s, 2)], d4s.at[s], d4q.at[me_s], "station", s)
 
     @pl.when(diag_owner)
     def _():
         for s in sp:
             diag_to_station(s).start()
-        dall[me_s] = own[NG]
+        dall[me_x, me_c, lax.rem(me_s, 2)] = own[NG]
 
     seg[me_s] = own[me_g]
     for i in range(16):
@@ -402,9 +417,8 @@
 
         @pl.when(x != me_s)
         def _():
-            arrived(own.at[NG], dall.at[x], d4s.at[0], d4q.at[x], "station", x)
-
-    pair = pl.ds(2 * me_g, 2)
+            arrived(own.at[NG], dall.at[me_x, me_c, h], d4s.at[0], d4q.at[x], "station", x)
+
     for i, x0 in enumerate(near_first):
         for dx in range(XC):
             x = x0 + dx
@@ -414,23 +428,33 @@
                 arrived(own.at[me_g], seg.at[x], s4.at[0], q4.at[x], "station", x)
 
         xs = pl.ds(x0, XC)
-        for g in gp:
-            send(seg.at[xs], call.at[me_g, xs], s5.at[i, g], q5.at[i, me_g], "group", g)
+        for p in xp:
+            send(seg.at[xs], call.at[me_c, me_x, xs], s5.at[i, p], q5.at[i, me_x], "group", 2 * p + me_c)
         if i == 0:
-            for g in gp:
-                send(dall.at[pair], dall.at[pair], d5s.at[g], d5q.at[me_g], "group", g)
-    call[me_g] = seg[...]
-    for g in gp:
-        gpair = pl.ds(2 * g, 2)
-        arrived(dall.at[gpair], dall.at[gpair], d5s.at[g], d5q.at[g], "group", g)
+            for p in xp:
+                send(dall.at[me_x, me_c], dall.at[me_x, me_c], d5s.at[p], d5q.at[me_x], "group", 2 * p + me_c)
+    call[me_c, me_x] = seg[...]
+
+    def forward(i):
+        xs = pl.ds(near_first[i], XC)
+        for p in xp:
+            arrived(seg.at[xs], call.at[me_c, p, xs], s5.at[i, p], q5.at[i, p], "group", 2 * p + me_c)
+        send(call.at[me_c, :, xs], call.at[me_c, :, xs], s7.at[i], q7.at[i], "group", mate)
+
+    for p in xp:
+        arrived(dall.at[p, me_c], dall.at[p, me_c], d5s.at[p], d5q.at[p], "group", 2 * p + me_c)
+    send(dall.at[:, me_c], dall.at[:, me_c], d7s, d7q, "group", mate)
+    forward(0)
+    arrived(dall.at[:, 1 - me_c], dall.at[:, 1 - me_c], d7s, d7q, "group", mate)
     for i, x0 in enumerate(near_first):
         xs = pl.ds(x0, XC)
-        for g in gp:
-            arrived(seg.at[xs], call.at[g, xs], s5.at[i, g], q5.at[i, g], "group", g)
+        if i + 1 < CH:
+            forward(i + 1)
+        arrived(call.at[1 - me_c, :, xs], call.at[1 - me_c, :, xs], s7.at[i], q7.at[i], "group", mate)
         for dx in range(XC):
             x = x0 + dx
             sg = [s2[s, slot[s, x]] for s in range(S)]
-            c = unpack_half(jnp.concatenate([call[g, x] for g in range(NG)], axis=0), dall[x])
+            c = unpack_half(jnp.concatenate([call[g % 2, g // 2, x] for g in range(NG)], axis=0), dall[x // 4, lax.rem(x // 2, 2), lax.rem(x, 2)])
             c2 = jnp.concatenate(split2(c), axis=1)
             c4 = jnp.concatenate([c2, c2], axis=0)
             out = jnp.dot(jnp.concatenate(sg, axis=0), c4, preferred_element_type=F32)
@@ -496,6 +520,10 @@
             diag_to_station(s).wait_send()
 
 
+def hbm(x):
+    return pltpu.with_memory_space_constraint(x, pltpu.HBM)
+
+
 def local(normal_mat, coupling, lengths, visible, bias_prior, unimod):
     vm = pl.BlockSpec(memory_space=pltpu.VMEM)
     sm = pl.BlockSpec(memory_space=pltpu.SMEM)
@@ -505,6 +533,7 @@
     slots = vmem((S, VH + 1, A, 2 * BS), BF16)
     wide = vmem((S, 2 * A, NH * BS), BF16)
     rows = vmem((NH, 8, BS), F32)
+    quart = vmem((4, NH, 8, BS), F32)
     half = vmem((S, HALF, BS), F32)
     cov, amb = pl.pallas_call(
         body,
@@ -519,9 +548,10 @@
             slots, slots, slots,
             pltpu.SMEM((S, NH), I32),
             vmem((S, A, A), F32),
-            vmem((NG, NH, 8, BS), F32),
+            vmem((2, 4, NH, 8, BS), F32),
             vmem((NH + 1, 8, BS), F32),
-            vmem((NG, NH + 1, 8, BS), F32),
+            quart, quart, quart,
+            vmem((NG, 8, BS), F32),
             vmem((NH + 2, 8, BS), F32),
             rows, rows,
             vmem((8, BS), F32),
@@ -529,27 +559,28 @@
             vmem((8, BS), F32),
             vmem((NG + 1, 8, BS), F32),
             rows,
-            vmem((NG, NH, 8, BS), F32),
-            rows,
+            vmem((2, 4, NH, 8, BS), F32),
+            vmem((4, 2, 2, 8, BS), F32),
             wide, wide,
             half, half,
             dma((2 + S,)),
-            dma((CH + 1, NG)), dma((CH + 1, NG)),
+            dma((CH,)), dma((CH,)), dma((CH, 4)), dma((CH, 4)), dma((NG,)), dma((NG,)),
             dma((NST,)), dma((NST,)), dma((2,)), dma((NST,)),
             dma((NG,)), dma((NG,)), dma((NG,)), dma((1,)),
             dma((NST,)), dma((NST,)), dma((NST,)), dma((NST,)),
-            dma((CH, NG)), dma((CH, NG)), dma((NG,)), dma((NG,)),
+            dma((CH, 4)), dma((CH, 4)), dma((4,)), dma((4,)),
+            dma((CH,)), dma((CH,)), dma(()), dma(()),
             dma((2,)), dma((2,)),
         ],
         compiler_params=pltpu.CompilerParams(vmem_limit_bytes=VMEM_LIMIT, collective_id=0, has_side_effects=True),
         name="epoch",
     )(
-        lengths,
-        visible.reshape(S, VH),
-        bias_prior.reshape(1, BS),
-        normal_mat,
-        coupling.reshape(S, VH, A, BS),
-        unimod,
+        hbm(lengths),
+        hbm(visible.reshape(S, VH)),
+        hbm(bias_prior.reshape(1, BS)),
+        hbm(normal_mat),
+        hbm(coupling.reshape(S, VH, A, BS)),
+        hbm(unimod),
     )
     return (cov.reshape(1, 1, BS, BS), amb)
 

time: 62.9 us -> 59.3 us (0.943)
  Pallas kernels: 59.1 us -> 57.2 us
  local copies, waits for them, and re-layouts: 2.99 us -> 1.26 us
    pallas_call x1, Pallas kernels: 59.1 us -> 57.2 us  [local(): pl.pallas_call(body, out_shape=(jax.ShapeDtypeStruct((BS, BS), F32), jax....]
    unnamed x2, local copies, waits for them, and re-layouts: 2.99 us -> 1.26 us
where the time goes in v4:
time: 59.3 us; the launch traced here: 59.1 us
  Pallas kernels  57.2 us (96%)
  local copies, waits for them, and re-layouts  1.26 us (2%)
  between operations  0.64 us (1%)
    pallas_call x1, Pallas kernels, local(): pl.pallas_call(body, out_shape=(jax.ShapeDtypeStruct((BS, BS), F32), jax....  57.2 us
    unnamed x2, local copies, waits for them, and re-layouts  1.26 us

profile of v4, /device:TPU:1, one launch (start us, length us, event | category | flops | bytes accessed | tf_op | source)
XLA Modules:
  0.0 59.1 jit_solution(10382126977198936597)
XLA Ops:
  0.6 57.2 %epoch.1 = (f32[128,128]{1,0:T(8,128)S(1)}, f32[8,2304]{1,0:T(8,128)S(1)}) custom-call(s32[8]{0:T(128)} %len_ref.1, s32[8,8]{1,0:T(8,128)} %bitcast.6, f32[1,128]{1,0:T(1,128)} %bitcast.7, f32[8,2304]{1,0:T(8,128)} %nm_hbm.1, f32[8,8,48,128]{3,2,1,0:T(8,128)} %bitcast.5, s32[8,2304]{1,0:T(8,128)} %um_hbm.1), custom_call_target="tpu_custom_call" | custom-call | tf_op jit(solution)/shard_map/epoch/pallas_call | solution.py:538
  57.9 0.6 %copy.10 = f32[1,1,128,128]{3,2,1,0:T(8,128)} copy(f32[1,1,128,128]{3,2,1,0:T(8,128)S(1)} %bitcast.4) | data formatting | bytes 131072
  58.5 0.6 %copy.11 = f32[8,2304]{1,0:T(8,128)} copy(f32[8,2304]{1,0:T(8,128)S(1)} %get-tuple-element.9) | data formatting | bytes 147456

commit v5 on v4

--- a/solution.py
+++ b/solution.py
@@ -71,15 +71,6 @@
     return out
 
 
-def scaled_rows(pinv, rows, col, k):
-    inside = (col >= k) & (col < k + 4)
-    rows = [jnp.where(inside, (col == k + q).astype(F32), rows[q]) for q in range(4)]
-    out = []
-    for q in range(4):
-        out.append((pinv[q][0] * rows[0] + pinv[q][1] * rows[1]) + (pinv[q][2] * rows[2] + pinv[q][3] * rows[3]))
-    return inside, out
-
-
 def unpack_rows(ref, base):
     lane = lanes_of()
     vregs = [ref[:, 128 * v : 128 * (v + 1)] for v in range(18)]
@@ -100,45 +91,6 @@
     return out
 
 
-def len_column(len_ref):
-    sub = subs_of()
-    out = jnp.zeros((8, 128), I32)
-    for s in range(S):
-        out = jnp.where(sub == s, len_ref[s], out)
-    return out
-
-
-def invert48(rows, lens):
-    lane = lanes_of()
-    col = lane & 63
-    side = lane & 64
-    m = []
-    for r in range(HALF):
-        row_id = jnp.where(lane < 64, r, r + HALF)
-        m.append(jnp.where((row_id < lens) & (col < lens), rows[r], (col == row_id).astype(F32)))
-    for k in range(0, A, 4):
-        high = k >= HALF
-        r0 = k % HALF
-        base = 64 if high else 0
-        dup = col + base
-        piv = [m[r0 + q] for q in range(4)]
-        p = [[pick(piv[q], jnp.full((8, 128), base + k + r, I32)) for r in range(4)] for q in range(4)]
-        pinv = inv4(p)
-        inside, rh = scaled_rows(pinv, [pick(piv[q], dup) for q in range(4)], col, k)
-        idx = [side + (k + q) for q in range(4)]
-        own_half = (lane >= 64) if high else (lane < 64)
-        new = []
-        for r in range(HALF):
-            c = [pick(m[r], idx[q]) for q in range(4)]
-            upd = (c[0] * rh[0] + c[1] * rh[1]) + (c[2] * rh[2] + c[3] * rh[3])
-            v = jnp.where(inside, 0.0, m[r]) - upd
-            if r0 <= r < r0 + 4:
-                v = jnp.where(own_half, rh[r - r0], v)
-            new.append(v)
-        m = new
-    return m
-
-
 def to_stations(m, buf):
     for r in range(HALF):
         buf[8 * r : 8 * r + 8, :] = m[r]
@@ -149,27 +101,94 @@
     return buf[pl.ds(s, A, stride=S), :][:, :A]
 
 
-def invert128(mat):
+def block_rows(pinv, rows):
+    return [(pinv[q][0] * rows[0] + pinv[q][1] * rows[1]) + (pinv[q][2] * rows[2] + pinv[q][3] * rows[3]) for q in range(4)]
+
+
+def regroup(tiles, shifts, width):
+    lane = lanes_of()
+    out = None
+    for h, (tile, shift) in enumerate(zip(tiles, shifts)):
+        shift = shift % 128
+        tile = pltpu.roll(tile, shift, 1) if shift else tile
+        out = tile if out is None else jnp.where(lane >= width * h, tile, out)
+    return out
+
+
+def eliminate(m, order, group, row_tile, row_lanes):
     lane = lanes_of()
     sub = subs_of()
-    m = list(mat)
-    for k in range(0, BS, 4):
-        t, o = divmod(k, 8)
-        rows = [jnp.broadcast_to(m[t][o + q : o + q + 1, :], (8, 128)) for q in range(4)]
-        at = [jnp.full((8, 128), k + q, I32) for q in range(4)]
-        p = [[pick(rows[q], at[r]) for r in range(4)] for q in range(4)]
-        inside, rh = scaled_rows(inv4(p), rows, lane, k)
+    jj = lane & (group - 1)
+    base = lane - jj
+    for k in range(0, order, 4):
+        u0, o = row_tile(k)
+        c0, j0 = divmod(k, group)
+        at = [base + (j0 + q) for q in range(4)]
+        inside = (jj >= j0) & (jj < j0 + 4)
+        wide = [[jnp.broadcast_to(t[o + q : o + q + 1, :], (8, 128)) for t in m[u0]] for q in range(4)]
+        h0 = row_lanes(k)
+        if h0 is None:
+            own = None
+            p = [[pick(wide[q][c0], at[r]) for r in range(4)] for q in range(4)]
+        else:
+            own = base == h0
+            p = [[pick(wide[q][c0], jnp.full((8, 128), h0 + j0 + r, I32)) for r in range(4)] for q in range(4)]
+            wide = [[pick(t, jj + h0) for t in row] for row in wide]
+        pinv = inv4(p)
+        rh = []
+        for c in range(len(m[0])):
+            rows = [wide[q][c] for q in range(4)]
+            if c == c0:
+                rows = [jnp.where(inside, (jj == j0 + q).astype(F32), rows[q]) for q in range(4)]
+            rh.append(block_rows(pinv, rows))
         new = []
-        for i in range(16):
-            c = [pick(m[i], at[q]) for q in range(4)]
-            upd = (c[0] * rh[0] + c[1] * rh[1]) + (c[2] * rh[2] + c[3] * rh[3])
-            v = jnp.where(inside, 0.0, m[i]) - upd
-            if i == t:
-                for q in range(4):
-                    v = jnp.where(sub == o + q, rh[q], v)
-            new.append(v)
+        for u in range(len(m)):
+            col = [pick(m[u][c0], at[q]) for q in range(4)]
+            line = []
+            for c in range(len(m[0])):
+                r = rh[c]
+                upd = (col[0] * r[0] + col[1] * r[1]) + (col[2] * r[2] + col[3] * r[3])
+                v = (jnp.where(inside, 0.0, m[u][c]) if c == c0 else m[u][c]) - upd
+                if u == u0:
+                    for q in range(4):
+                        hit = sub == o + q
+                        v = jnp.where(hit if own is None else hit & own, r[q], v)
+                line.append(v)
+            new.append(line)
         m = new
     return m
+
+
+def invert48(buf, len_ref):
+    lane = lanes_of()
+    sub = subs_of()
+    lens = jnp.zeros((8, 128), I32)
+    for s in range(S):
+        lens = jnp.where(lane >= 16 * s, len_ref[s], lens)
+    nat = [buf[pl.ds(s, A, stride=S), :] for s in range(S)]
+    m = []
+    for t in range(6):
+        line = []
+        for c in range(3):
+            v = regroup([nat[s][8 * t : 8 * t + 8] for s in range(S)], [16 * s - 16 * c for s in range(S)], 16)
+            row, col = sub + 8 * t, (lane & 15) + 16 * c
+            line.append(jnp.where((row < lens) & (col < lens), v, (row == col).astype(F32)))
+        m.append(line)
+    m = eliminate(m, A, 16, lambda k: (k // 8, k % 8), lambda k: None)
+    out = []
+    for s in range(S):
+        tiles = []
+        for t in range(6):
+            v = regroup(m[t], [16 * c - 16 * s for c in range(3)], 16)
+            tiles.append(jnp.where(lane < A, v, 0.0))
+        out.append(jnp.concatenate(tiles, axis=0))
+    return out
+
+
+def invert128(mat):
+    m = [[regroup([mat[4 * u + h] for h in range(4)], [32 * h - 32 * c for h in range(4)], 32) for c in range(4)] for u in range(4)]
+    m = eliminate(m, BS, 32, lambda k: (k // 32, k % 8), lambda k: 32 * ((k // 8) % 4))
+    return [regroup(m[i // 4], [32 * c - 32 * (i % 4) for c in range(4)], 32) for i in range(16)]
 
 
 def peer(axis, index):
@@ -253,13 +272,13 @@
     near_first = [lax.rem(near + XC * d, NH) for d in (0, 1, 3, 2)]
     diag_owner = me_g == me_s // 2
 
-    lens = len_column(len_ref)
 
     nm_copy.wait()
-    to_stations(invert48(unpack_rows(nm, 0), lens), buf)
+    to_stations(unpack_rows(nm, 0), buf)
+    inverses = invert48(buf, len_ref)
     zeros = jnp.zeros((A, 2 * BS), BF16)
     for s in range(S):
-        inv = station(buf, s)
+        inv = inverses[s][:, :A]
         invs[s] = inv
         lhs = jnp.concatenate(split2(inv), axis=0)
         keep = lax.broadcasted_iota(I32, (A, BS), 0) < len_ref[s]

time: 59.3 us -> 57.8 us (0.975)
  Pallas kernels: 57.2 us -> 55.7 us
    pallas_call x1, Pallas kernels: 57.2 us -> 55.7 us  [local(): pl.pallas_call(body, out_shape=(jax.ShapeDtypeStruct((BS, BS), F32), jax....]
where the time goes in v5:
time: 57.8 us; the launch traced here: 57.6 us
  Pallas kernels  55.7 us (96%)
  local copies, waits for them, and re-layouts  1.26 us (2%)
  between operations  0.64 us (1%)
    pallas_call x1, Pallas kernels, local(): pl.pallas_call(body, out_shape=(jax.ShapeDtypeStruct((BS, BS), F32), jax....  55.7 us
    unnamed x2, local copies, waits for them, and re-layouts  1.26 us

profile of v5, /device:TPU:1, one launch (start us, length us, event | category | flops | bytes accessed | tf_op | source)
XLA Modules:
  0.0 57.6 jit_solution(10887326769411450414)
XLA Ops:
  0.6 55.7 %epoch.1 = (f32[128,128]{1,0:T(8,128)S(1)}, f32[8,2304]{1,0:T(8,128)S(1)}) custom-call(s32[8]{0:T(128)} %len_ref.1, s32[8,8]{1,0:T(8,128)} %bitcast.6, f32[1,128]{1,0:T(1,128)} %bitcast.7, f32[8,2304]{1,0:T(8,128)} %nm_hbm.1, f32[8,8,48,128]{3,2,1,0:T(8,128)} %bitcast.5, s32[8,2304]{1,0:T(8,128)} %um_hbm.1), custom_call_target="tpu_custom_call" | custom-call | tf_op jit(solution)/shard_map/epoch/pallas_call | solution.py:557
  56.4 0.6 %copy.10 = f32[1,1,128,128]{3,2,1,0:T(8,128)} copy(f32[1,1,128,128]{3,2,1,0:T(8,128)S(1)} %bitcast.4) | data formatting | bytes 131072
  57.0 0.6 %copy.11 = f32[8,2304]{1,0:T(8,128)} copy(f32[8,2304]{1,0:T(8,128)S(1)} %get-tuple-element.9) | data formatting | bytes 147456

commit v6 on v5

--- a/solution.py
+++ b/solution.py
@@ -38,39 +38,6 @@
     return hi, lo
 
 
-def inv2(m):
-    (a, b), (c, d) = m
-    r = 1.0 / (a * d - b * c)
-    return [[d * r, -(b * r)], [-(c * r), a * r]]
-
-
-def mul2(m, n):
-    return [[m[i][0] * n[0][j] + m[i][1] * n[1][j] for j in range(2)] for i in range(2)]
-
-
-def inv4(p):
-    a = [[p[i][j] for j in range(2)] for i in range(2)]
-    b = [[p[i][j + 2] for j in range(2)] for i in range(2)]
-    c = [[p[i + 2][j] for j in range(2)] for i in range(2)]
-    d = [[p[i + 2][j + 2] for j in range(2)] for i in range(2)]
-    ai = inv2(a)
-    t = mul2(ai, b)
-    u = mul2(c, ai)
-    ct = mul2(c, t)
-    si = inv2([[d[i][j] - ct[i][j] for j in range(2)] for i in range(2)])
-    ts = mul2(t, si)
-    su = mul2(si, u)
-    tsu = mul2(ts, u)
-    out = [[None] * 4 for _ in range(4)]
-    for i in range(2):
-        for j in range(2):
-            out[i][j] = ai[i][j] + tsu[i][j]
-            out[i][j + 2] = -ts[i][j]
-            out[i + 2][j] = -su[i][j]
-            out[i + 2][j + 2] = si[i][j]
-    return out
-
-
 def unpack_rows(ref, base):
     lane = lanes_of()
     vregs = [ref[:, 128 * v : 128 * (v + 1)] for v in range(18)]
@@ -101,8 +68,26 @@
     return buf[pl.ds(s, A, stride=S), :][:, :A]
 
 
-def block_rows(pinv, rows):
-    return [(pinv[q][0] * rows[0] + pinv[q][1] * rows[1]) + (pinv[q][2] * rows[2] + pinv[q][3] * rows[3]) for q in range(4)]
+def pivot_terms(p):
+    a, b, d = p[0][0], p[0][1], p[1][1]
+    det = a * d - b * b
+    u = [[d * p[0][j] - b * p[1][j] for j in (2, 3)], [a * p[1][j] - b * p[0][j] for j in (2, 3)]]
+    s00 = det * p[2][2] - (p[0][2] * u[0][0] + p[1][2] * u[1][0])
+    s01 = det * p[2][3] - (p[0][2] * u[0][1] + p[1][2] * u[1][1])
+    s11 = det * p[3][3] - (p[0][3] * u[0][1] + p[1][3] * u[1][1])
+    r = 1.0 / det
+    q = det * (1.0 / (s00 * s11 - s01 * s01))
+    t = [[v * r for v in row] for row in u]
+    return (a * r, b * r, d * r), t, (s00, s01, s11), q
+
+
+def pivot_rows(terms, rows):
+    (ar, br, dr), t, (s00, s01, s11), q = terms
+    w = [rows[2 + j] - (t[0][j] * rows[0] + t[1][j] * rows[1]) for j in range(2)]
+    y2 = [q * (s11 * w[0] - s01 * w[1]), q * (s00 * w[1] - s01 * w[0])]
+    v = [dr * rows[0] - br * rows[1], ar * rows[1] - br * rows[0]]
+    y1 = [v[i] - (t[i][0] * y2[0] + t[i][1] * y2[1]) for i in range(2)]
+    return y1 + y2
 
 
 def regroup(tiles, shifts, width):
@@ -127,28 +112,29 @@
         inside = (jj >= j0) & (jj < j0 + 4)
         wide = [[jnp.broadcast_to(t[o + q : o + q + 1, :], (8, 128)) for t in m[u0]] for q in range(4)]
         h0 = row_lanes(k)
-        if h0 is None:
-            own = None
-            p = [[pick(wide[q][c0], at[r]) for r in range(4)] for q in range(4)]
-        else:
-            own = base == h0
-            p = [[pick(wide[q][c0], jnp.full((8, 128), h0 + j0 + r, I32)) for r in range(4)] for q in range(4)]
+        own = None if h0 is None else base == h0
+        p = [[None] * 4 for _ in range(4)]
+        for q in range(4):
+            for r in range(q, 4):
+                to = at[r] if h0 is None else jnp.full((8, 128), h0 + j0 + r, I32)
+                p[q][r] = p[r][q] = pick(wide[q][c0], to)
+        if h0 is not None:
             wide = [[pick(t, jj + h0) for t in row] for row in wide]
-        pinv = inv4(p)
+        terms = pivot_terms(p)
         rh = []
         for c in range(len(m[0])):
             rows = [wide[q][c] for q in range(4)]
             if c == c0:
                 rows = [jnp.where(inside, (jj == j0 + q).astype(F32), rows[q]) for q in range(4)]
-            rh.append(block_rows(pinv, rows))
+            rh.append(pivot_rows(terms, rows))
         new = []
         for u in range(len(m)):
             col = [pick(m[u][c0], at[q]) for q in range(4)]
             line = []
             for c in range(len(m[0])):
                 r = rh[c]
-                upd = (col[0] * r[0] + col[1] * r[1]) + (col[2] * r[2] + col[3] * r[3])
-                v = (jnp.where(inside, 0.0, m[u][c]) if c == c0 else m[u][c]) - upd
+                v = jnp.where(inside, 0.0, m[u][c]) if c == c0 else m[u][c]
+                v = (v - (col[2] * r[2] + col[3] * r[3])) - (col[0] * r[0] + col[1] * r[1])
                 if u == u0:
                     for q in range(4):
                         hit = sub == o + q

time: 57.8 us -> 56.9 us (0.984)
  Pallas kernels: 55.7 us -> 54.8 us
    pallas_call x1, Pallas kernels: 55.7 us -> 54.8 us  [local(): pl.pallas_call(body, out_shape=(jax.ShapeDtypeStruct((BS, BS), F32), jax....]
where the time goes in v6:
time: 56.9 us; the launch traced here: 56.8 us
  Pallas kernels  54.8 us (96%)
  local copies, waits for them, and re-layouts  1.26 us (2%)
  between operations  0.64 us (1%)
    pallas_call x1, Pallas kernels, local(): pl.pallas_call(body, out_shape=(jax.ShapeDtypeStruct((BS, BS), F32), jax....  54.8 us
    unnamed x2, local copies, waits for them, and re-layouts  1.26 us

profile of v6, /device:TPU:1, one launch (start us, length us, event | category | flops | bytes accessed | tf_op | source)
XLA Modules:
  0.0 56.8 jit_solution(2966501522093581597)
XLA Ops:
  0.6 54.8 %epoch.1 = (f32[128,128]{1,0:T(8,128)S(1)}, f32[8,2304]{1,0:T(8,128)S(1)}) custom-call(s32[8]{0:T(128)} %len_ref.1, s32[8,8]{1,0:T(8,128)} %bitcast.6, f32[1,128]{1,0:T(1,128)} %bitcast.7, f32[8,2304]{1,0:T(8,128)} %nm_hbm.1, f32[8,8,48,128]{3,2,1,0:T(8,128)} %bitcast.5, s32[8,2304]{1,0:T(8,128)} %um_hbm.1), custom_call_target="tpu_custom_call" | custom-call | tf_op jit(solution)/shard_map/epoch/pallas_call | solution.py:543
  55.5 0.6 %copy.10 = f32[1,1,128,128]{3,2,1,0:T(8,128)} copy(f32[1,1,128,128]{3,2,1,0:T(8,128)S(1)} %bitcast.4) | data formatting | bytes 131072
  56.1 0.6 %copy.11 = f32[8,2304]{1,0:T(8,128)} copy(f32[8,2304]{1,0:T(8,128)S(1)} %get-tuple-element.9) | data formatting | bytes 147456

commit v7 on v6

--- a/solution.py
+++ b/solution.py
@@ -181,8 +181,10 @@
     return {axis: index}
 
 
-CH = 4
-XC = NH // CH
+CR = 2
+XR = NH // CR
+CG = 2
+XG = NH // CG
 HB = BS // 2
 
 
@@ -253,9 +255,8 @@
 
     lane = lanes_of()
     sub = subs_of()
-    near = XC * (me_s // XC)
-    far_first = [lax.rem(near + XC * d, NH) for d in (2, 1, 3, 0)]
-    near_first = [lax.rem(near + XC * d, NH) for d in (0, 1, 3, 2)]
+    far_first = [lax.rem(XR * (me_s // XR) + XR * d, NH) for d in range(CR - 1, -1, -1)]
+    near_first = [lax.rem(XG * (me_s // XG) + XG * d, NH) for d in range(CG)]
     diag_owner = me_g == me_s // 2
 
 
@@ -283,14 +284,14 @@
         s2[s, VH] = zeros
 
     def pass_on(i):
-        xs = pl.ds(far_first[i], XC)
+        xs = pl.ds(far_first[i], XR)
         arrived(table.at[me_c, :, xs], rc.at[:, xs], sa.at[i], qa.at[i], "group", mate)
         tsum[:, xs] = table[me_c, :, xs] + rc[:, xs]
         for p in xp:
             send(tsum.at[p, xs], r1.at[me_x, xs], s1.at[i, p], q1.at[i, me_x], "group", 2 * p + me_c)
 
     for i, x0 in enumerate(far_first):
-        for dx in range(XC):
+        for dx in range(XR):
             x = x0 + dx
             at = []
             for s in range(S):
@@ -310,7 +311,7 @@
             ediag[x] = diag_tile(out[:HB])
         if i == 0:
             pl.semaphore_wait(barrier, NG - 1 + NST - 1 + 1)
-        xs = pl.ds(x0, XC)
+        xs = pl.ds(x0, XR)
         send(table.at[1 - me_c, :, xs], rc.at[:, xs], sa.at[i], qa.at[i], "group", mate)
         if i > 0:
             pass_on(i - 1)
@@ -322,19 +323,19 @@
     ediag[NH] = both
     for g in gp:
         send(ediag.at[NH], rd1.at[me_g], d1s.at[g], d1q.at[me_g], "group", g)
-    pass_on(CH - 1)
+    pass_on(CR - 1)
 
     def to_owner(x):
         return remote(part.at[x], r2.at[me_s], s2s.at[x], q2.at[me_s], "station", x)
 
     for i, x0 in enumerate(far_first):
-        xs = pl.ds(x0, XC)
+        xs = pl.ds(x0, XR)
         total = tsum[me_x, xs]
         for p in xp:
             arrived(tsum.at[p, xs], r1.at[p, xs], s1.at[i, p], q1.at[i, p], "group", 2 * p + me_c)
             total = total + r1[p, xs]
         part[xs] = total
-        for dx in range(XC):
+        for dx in range(XR):
             x = x0 + dx
 
             @pl.when(x != me_s)
@@ -425,14 +426,14 @@
             arrived(own.at[NG], dall.at[me_x, me_c, h], d4s.at[0], d4q.at[x], "station", x)
 
     for i, x0 in enumerate(near_first):
-        for dx in range(XC):
+        for dx in range(XG):
             x = x0 + dx
 
             @pl.when(x != me_s)
             def _():
                 arrived(own.at[me_g], seg.at[x], s4.at[0], q4.at[x], "station", x)
 
-        xs = pl.ds(x0, XC)
+        xs = pl.ds(x0, XG)
         for p in xp:
             send(seg.at[xs], call.at[me_c, me_x, xs], s5.at[i, p], q5.at[i, me_x], "group", 2 * p + me_c)
         if i == 0:
@@ -441,7 +442,7 @@
     call[me_c, me_x] = seg[...]
 
     def forward(i):
-        xs = pl.ds(near_first[i], XC)
+        xs = pl.ds(near_first[i], XG)
         for p in xp:
             arrived(seg.at[xs], call.at[me_c, p, xs], s5.at[i, p], q5.at[i, p], "group", 2 * p + me_c)
         send(call.at[me_c, :, xs], call.at[me_c, :, xs], s7.at[i], q7.at[i], "group", mate)
@@ -451,12 +452,15 @@
     send(dall.at[:, me_c], dall.at[:, me_c], d7s, d7q, "group", mate)
     forward(0)
     arrived(dall.at[:, 1 - me_c], dall.at[:, 1 - me_c], d7s, d7q, "group", mate)
+    nt = (((1,), (1,)), ((), ()))
+    partial = [None] * S
+    pad = jnp.zeros((HALF, 64 - A), F32)
     for i, x0 in enumerate(near_first):
-        xs = pl.ds(x0, XC)
-        if i + 1 < CH:
+        xs = pl.ds(x0, XG)
+        if i + 1 < CG:
             forward(i + 1)
         arrived(call.at[1 - me_c, :, xs], call.at[1 - me_c, :, xs], s7.at[i], q7.at[i], "group", mate)
-        for dx in range(XC):
+        for dx in range(XG):
             x = x0 + dx
             sg = [s2[s, slot[s, x]] for s in range(S)]
             c = unpack_half(jnp.concatenate([call[g % 2, g // 2, x] for g in range(NG)], axis=0), dall[x // 4, lax.rem(x // 2, 2), lax.rem(x, 2)])
@@ -464,23 +468,24 @@
             c4 = jnp.concatenate([c2, c2], axis=0)
             out = jnp.dot(jnp.concatenate(sg, axis=0), c4, preferred_element_type=F32)
             hi, lo = split2(out[:, :BS] + out[:, BS:])
-            n = XC * i + dx
+            n = XG * i + dx
             at = slice(BS * n, BS * n + BS)
             for s in range(S):
                 sx[s, :A, at] = sg[s][:, :BS]
                 sx[s, A:, at] = sg[s][:, BS:]
                 lx[s, :A, at] = hi[A * s : A * s + A]
                 lx[s, A:, at] = lo[A * s : A * s + A]
-    nt = (((1,), (1,)), ((), ()))
-    pad = jnp.zeros((HALF, 64 - A), F32)
-    for s in range(S):
-        out = lax.dot_general(lx[s], sx[s], nt, preferred_element_type=F32)
-        out = out[:A] + out[A:]
-        out = out[:, :A] + out[:, A:]
-        mine[s] = jnp.concatenate([out[:HALF], pad, out[HALF:], pad], axis=1)
-        if s % 4 == 3:
-            ss = pl.ds(s - 3, 4)
-            send(mine.at[ss], theirs.at[ss], s6.at[s // 4], q6.at[s // 4], "bias", 1 - me_b)
+        for s in range(S):
+            at = slice(BS * XG * i, BS * XG * (i + 1))
+            out = lax.dot_general(lx[s, :, at], sx[s, :, at], nt, preferred_element_type=F32)
+            out = out[:A] + out[A:]
+            out = out[:, :A] + out[:, A:]
+            partial[s] = out if i == 0 else partial[s] + out
+            if i == CG - 1:
+                mine[s] = jnp.concatenate([partial[s][:HALF], pad, partial[s][HALF:], pad], axis=1)
+                if s % 4 == 3:
+                    ss = pl.ds(s - 3, 4)
+                    send(mine.at[ss], theirs.at[ss], s6.at[s // 4], q6.at[s // 4], "bias", 1 - me_b)
     ri = lax.broadcasted_iota(I32, (A, A), 0)
     ci = lax.broadcasted_iota(I32, (A, A), 1)
     for s in range(S):
@@ -569,12 +574,12 @@
             wide, wide,
             half, half,
             dma((2 + S,)),
-            dma((CH,)), dma((CH,)), dma((CH, 4)), dma((CH, 4)), dma((NG,)), dma((NG,)),
+            dma((CR,)), dma((CR,)), dma((CR, 4)), dma((CR, 4)), dma((NG,)), dma((NG,)),
             dma((NST,)), dma((NST,)), dma((2,)), dma((NST,)),
             dma((NG,)), dma((NG,)), dma((NG,)), dma((1,)),
             dma((NST,)), dma((NST,)), dma((NST,)), dma((NST,)),
-            dma((CH, 4)), dma((CH, 4)), dma((4,)), dma((4,)),
-            dma((CH,)), dma((CH,)), dma(()), dma(()),
+            dma((CG, 4)), dma((CG, 4)), dma((4,)), dma((4,)),
+            dma((CG,)), dma((CG,)), dma(()), dma(()),
             dma((2,)), dma((2,)),
         ],
         compiler_params=pltpu.CompilerParams(vmem_limit_bytes=VMEM_LIMIT, collective_id=0, has_side_effects=True),

time: 56.9 us -> 56.9 us (level)
  no operation moved by 1% of the time
where the time goes in v7:
time: 56.9 us; the launch traced here: 56.8 us
  Pallas kernels  54.9 us (96%)
  local copies, waits for them, and re-layouts  1.26 us (2%)
  between operations  0.64 us (1%)
    pallas_call x1, Pallas kernels, local(): pl.pallas_call(body, out_shape=(jax.ShapeDtypeStruct((BS, BS), F32), jax....  54.9 us
    unnamed x2, local copies, waits for them, and re-layouts  1.26 us

profile of v7, /device:TPU:1, one launch (start us, length us, event | category | flops | bytes accessed | tf_op | source)
XLA Modules:
  0.0 56.8 jit_solution(6289819848542067889)
XLA Ops:
  0.6 54.9 %epoch.1 = (f32[128,128]{1,0:T(8,128)S(1)}, f32[8,2304]{1,0:T(8,128)S(1)}) custom-call(s32[8]{0:T(128)} %len_ref.1, s32[8,8]{1,0:T(8,128)} %bitcast.6, f32[1,128]{1,0:T(1,128)} %bitcast.7, f32[8,2304]{1,0:T(8,128)} %nm_hbm.1, f32[8,8,48,128]{3,2,1,0:T(8,128)} %bitcast.5, s32[8,2304]{1,0:T(8,128)} %um_hbm.1), custom_call_target="tpu_custom_call" | custom-call | tf_op jit(solution)/shard_map/epoch/pallas_call | solution.py:548
  55.5 0.6 %copy.10 = f32[1,1,128,128]{3,2,1,0:T(8,128)} copy(f32[1,1,128,128]{3,2,1,0:T(8,128)S(1)} %bitcast.4) | data formatting | bytes 131072
  56.2 0.6 %copy.11 = f32[8,2304]{1,0:T(8,128)} copy(f32[8,2304]{1,0:T(8,128)S(1)} %get-tuple-element.9) | data formatting | bytes 147456

commit v8 on v7

--- a/solution.py
+++ b/solution.py
@@ -452,9 +452,6 @@
     send(dall.at[:, me_c], dall.at[:, me_c], d7s, d7q, "group", mate)
     forward(0)
     arrived(dall.at[:, 1 - me_c], dall.at[:, 1 - me_c], d7s, d7q, "group", mate)
-    nt = (((1,), (1,)), ((), ()))
-    partial = [None] * S
-    pad = jnp.zeros((HALF, 64 - A), F32)
     for i, x0 in enumerate(near_first):
         xs = pl.ds(x0, XG)
         if i + 1 < CG:
@@ -475,17 +472,16 @@
                 sx[s, A:, at] = sg[s][:, BS:]
                 lx[s, :A, at] = hi[A * s : A * s + A]
                 lx[s, A:, at] = lo[A * s : A * s + A]
-        for s in range(S):
-            at = slice(BS * XG * i, BS * XG * (i + 1))
-            out = lax.dot_general(lx[s, :, at], sx[s, :, at], nt, preferred_element_type=F32)
-            out = out[:A] + out[A:]
-            out = out[:, :A] + out[:, A:]
-            partial[s] = out if i == 0 else partial[s] + out
-            if i == CG - 1:
-                mine[s] = jnp.concatenate([partial[s][:HALF], pad, partial[s][HALF:], pad], axis=1)
-                if s % 4 == 3:
-                    ss = pl.ds(s - 3, 4)
-                    send(mine.at[ss], theirs.at[ss], s6.at[s // 4], q6.at[s // 4], "bias", 1 - me_b)
+    nt = (((1,), (1,)), ((), ()))
+    pad = jnp.zeros((HALF, 64 - A), F32)
+    for s in range(S):
+        out = lax.dot_general(lx[s], sx[s], nt, preferred_element_type=F32)
+        out = out[:A] + out[A:]
+        out = out[:, :A] + out[:, A:]
+        mine[s] = jnp.concatenate([out[:HALF], pad, out[HALF:], pad], axis=1)
+        if s % 4 == 3:
+            ss = pl.ds(s - 3, 4)
+            send(mine.at[ss], theirs.at[ss], s6.at[s // 4], q6.at[s // 4], "bias", 1 - me_b)
     ri = lax.broadcasted_iota(I32, (A, A), 0)
     ci = lax.broadcasted_iota(I32, (A, A), 1)
     for s in range(S):

time: 56.9 us -> 56.2 us (0.988)
  Pallas kernels: 54.9 us -> 54.1 us
    pallas_call x1, Pallas kernels: 54.9 us -> 54.1 us  [local(): pl.pallas_call(body, out_shape=(jax.ShapeDtypeStruct((BS, BS), F32), jax....]
where the time goes in v8:
time: 56.2 us; the launch traced here: 56 us
  Pallas kernels  54.1 us (96%)
  local copies, waits for them, and re-layouts  1.26 us (2%)
  between operations  0.64 us (1%)
    pallas_call x1, Pallas kernels, local(): pl.pallas_call(body, out_shape=(jax.ShapeDtypeStruct((BS, BS), F32), jax....  54.1 us
    unnamed x2, local copies, waits for them, and re-layouts  1.26 us

profile of v8, /device:TPU:1, one launch (start us, length us, event | category | flops | bytes accessed | tf_op | source)
XLA Modules:
  0.0 56.0 jit_solution(16859548880836987789)
XLA Ops:
  0.6 54.1 %epoch.1 = (f32[128,128]{1,0:T(8,128)S(1)}, f32[8,2304]{1,0:T(8,128)S(1)}) custom-call(s32[8]{0:T(128)} %len_ref.1, s32[8,8]{1,0:T(8,128)} %bitcast.6, f32[1,128]{1,0:T(1,128)} %bitcast.7, f32[8,2304]{1,0:T(8,128)} %nm_hbm.1, f32[8,8,48,128]{3,2,1,0:T(8,128)} %bitcast.5, s32[8,2304]{1,0:T(8,128)} %um_hbm.1), custom_call_target="tpu_custom_call" | custom-call | tf_op jit(solution)/shard_map/epoch/pallas_call | solution.py:544
  54.7 0.6 %copy.10 = f32[1,1,128,128]{3,2,1,0:T(8,128)} copy(f32[1,1,128,128]{3,2,1,0:T(8,128)S(1)} %bitcast.4) | data formatting | bytes 131072
  55.4 0.6 %copy.11 = f32[8,2304]{1,0:T(8,128)} copy(f32[8,2304]{1,0:T(8,128)S(1)} %get-tuple-element.9) | data formatting | bytes 147456
